TPU v7x, 256 devices: a whole 4x4x8 slice. The times are simulated.
256 devices in a mesh: item: 8 (over z), user: 16 (over x, y), mp: 2 (over core).
Axes of the slice: x: 4, y: 4, z: 8, core: 2. Of those that a mesh axis runs over, the one named last changes fastest.
Arguments:
- item_last_hidden: bfloat16 [32768, 4096], P(('item', 'user'), 'mp'), may hold values from -6 to 6
- frozen_down_weight: bfloat16 [4096, 16], P('mp'), may hold values from -0.09375 to 0.09375
- trained_up_weight: bfloat16 [16, 4096], P(None, 'mp'), may hold values from -1.5 to 1.5
- embedding_norm_gain: float32 [4096], P('mp'), may hold values from 0.5 to 1.5
- user_context_state: bfloat16 [18432, 4096], P(('item', 'user'), 'mp'), may hold values from -110 to 110
- history_owner_device: int32 [18432, 1], P(('item', 'user')), may hold values from 0 to 127; in each aligned block of 144 rows (0 to 143, 144 to 287, ...) at most 2 rows name the same one
- history_item_row: int32 [18432], P(('item', 'user')), may hold values from 0 to 255
Outputs:
- pos_loss: float32 [18432], P(('item', 'user'))
- emb_grad: float32 [32768, 4096], P(('item', 'user'), 'mp')
- b_grad: float32 [16, 4096], P(None, 'mp')
Inputs may be any that keep to these rules, and one draw needn't show every extreme that they name: `history_owner_device`: within the rows of one device no owner appears more than 2 times, and some owner appears exactly 2 times.
All inputs are finite; a program needn't handle non-finite values.
Results may differ from a plain program's by a relative error of at most 0.012.
The roundings to bfloat16 on the way count: a program that leaves them out, or rounds other values in their place, can miss the bound.
Values may be sent and summed in bfloat16 or wider, within the bound.
No kernel may reach another device: no remote copies, remote signals or barrier semaphores. Data moves between devices by JAX's collectives and lax.ppermute only.
A program may use at most 64 MiB of HBM per device.

v0:
```python
import math

import jax
import jax.numpy as jnp
from jax import lax
from jax.sharding import PartitionSpec as P

MODEL_WIDTH = 4096
LEN = 48


EPS = 1e-06


def body(
    item_last_hidden,
    frozen_down_weight,
    trained_up_weight,
    embedding_norm_gain,
    user_context_state,
    history_owner_device,
    history_item_row,
):
    part_width = item_last_hidden.shape[1]
    stored = item_last_hidden.shape[0]
    low_rank_output = lax.psum(
        jnp.dot(item_last_hidden, frozen_down_weight, preferred_element_type=jnp.float32), "mp"
    )
    pre_norm_input = item_last_hidden.astype(jnp.float32) + jnp.dot(
        low_rank_output, trained_up_weight.astype(jnp.float32), precision=lax.Precision.HIGHEST
    )
    squares = lax.psum(jnp.sum(pre_norm_input * pre_norm_input, axis=1, keepdims=True), "mp")
    rinv = lax.rsqrt(squares / MODEL_WIDTH + EPS)
    emb = (pre_norm_input * rinv * embedding_norm_gain).astype(jnp.bfloat16)
    owners = history_owner_device[:, 0]
    count = history_item_row.shape[0]
    devices = lax.axis_size(("item", "user"))
    slots = max(2, 2 * count // devices)
    owner_table = (owners[:, None] == jnp.arange(devices, dtype=jnp.int32)[None, :]).astype(
        jnp.int32
    )
    ranks = jnp.sum((jnp.cumsum(owner_table, axis=0) - owner_table) * owner_table, axis=1)
    where_to = owners * slots + ranks
    wanted = (
        jnp.zeros((devices * slots,), jnp.int32)
        .at[where_to]
        .set(history_item_row)
        .reshape(devices, slots)
    )
    asked = lax.all_to_all(wanted, ("item", "user"), split_axis=0, concat_axis=0, tiled=True)
    found = emb[asked.reshape(-1)].reshape(asked.shape[0], asked.shape[1], part_width)
    fetched = lax.all_to_all(found, ("item", "user"), split_axis=0, concat_axis=0, tiled=True)
    hist = fetched.reshape(devices * slots, part_width)[where_to]
    users = lax.axis_size("user")
    me = lax.axis_index("user")
    group = users * count
    local = jnp.arange(count, dtype=jnp.int32)
    partial_scores = lax.dot_general(
        user_context_state,
        lax.all_gather(hist, "user", axis=0, tiled=True),
        (((1,), (1,)), ((), ())),
        preferred_element_type=jnp.float32,
    )
    scores = lax.psum(partial_scores, "mp") / math.sqrt(MODEL_WIDTH)
    top = jnp.max(scores, axis=1, keepdims=True)
    lse = top + jnp.log(jnp.sum(jnp.exp(scores - top), axis=1, keepdims=True))
    target = jnp.minimum(me * count + local + 1, group - 1)
    valid = local % LEN != LEN - 1
    positive = jnp.take_along_axis(scores, target[:, None], axis=1)
    pos_loss = jnp.where(valid, (lse - positive)[:, 0], 0.0)
    columns = jnp.arange(group, dtype=jnp.int32)
    hit = (columns[None, :] == target[:, None]).astype(jnp.float32)
    dscore = jnp.where(valid[:, None], jnp.exp(scores - lse) - hit, 0.0).astype(jnp.bfloat16)
    hist_grad = lax.psum_scatter(
        lax.dot_general(
            dscore, user_context_state, (((0,), (0,)), ((), ())), preferred_element_type=jnp.float32
        ).astype(jnp.bfloat16),
        "user",
        scatter_dimension=0,
        tiled=True,
    )
    outgoing = jnp.zeros((devices * slots, part_width), jnp.bfloat16).at[where_to].set(hist_grad)
    returned = lax.all_to_all(
        outgoing.reshape(devices, slots, part_width),
        ("item", "user"),
        split_axis=0,
        concat_axis=0,
        tiled=True,
    )
    picker = (jnp.arange(stored, dtype=jnp.int32)[:, None] == asked.reshape(1, -1)).astype(
        jnp.bfloat16
    )
    emb_grad = jnp.dot(
        picker, returned.reshape(devices * slots, part_width), preferred_element_type=jnp.float32
    )
    scaled = emb_grad * embedding_norm_gain
    inner = lax.psum(jnp.sum(pre_norm_input * scaled, axis=1, keepdims=True), "mp") / MODEL_WIDTH
    dpre = rinv * scaled - pre_norm_input * rinv * rinv * rinv * inner
    b_grad = lax.psum(
        jnp.dot(low_rank_output.T, dpre, precision=lax.Precision.HIGHEST), ("item", "user")
    )
    return (pos_loss, emb_grad, b_grad)


def solution(mesh):
    placed = (
        P(("item", "user"), "mp"),
        P("mp", None),
        P(None, "mp"),
        P("mp"),
        P(("item", "user"), "mp"),
        P(("item", "user"), None),
        P(("item", "user")),
    )
    return jax.shard_map(
        body,
        mesh=mesh,
        in_specs=placed,
        out_specs=(P(("item", "user")), P(("item", "user"), "mp"), P(None, "mp")),
        check_vma=False,
    )
```

profile of v0, /device:TPU:2, one launch (start us, length us, event | category | flops | bytes accessed | tf_op | source)
XLA Modules:
  0.0 580.1 jit_solution(13240151713814006992)
XLA Ops:
  7.2 0.9 iota_compare_fusion.3
  8.1 0.1 fusion.18
  8.3 0.9 fusion.22
  9.2 0.7 compare_select_fusion.2
  9.9 1.2 scatter_custom_fusion
  11.1 0.8 all_to_all.12
  11.9 15.4 %all-to-all-start = ((s32[128,1,2]{2,1,0:T(1,128)}), s32[128,1,2]{2,1,0:T(1,128)S(1)}, u32[]{:S(2)}, u32[]{:S(2)}) async-start(s32[128,1,2]{2,1,0:T(1,128)} %bitcast.9), calls=%async_computation | async-start | bytes 131072 | tf_op jit(solution)/shard_map/all_to_all | solution.py:50
  27.3 1.6 fusion.33
  28.9 3.4 psum.35
  32.3 2.5 multiply_reduce_fusion.1
  34.8 2.4 psum.36
  37.3 1.8 multiply_convert_fusion
  39.2 0.5 broadcast.227
  39.7 0.8 reduce.5
  40.5 0.1 reshape.140
  40.6 1.4 gather_fusion
  42.0 1.5 reshape.141
  43.5 13.7 %all-to-all-start.1 = ((bf16[128,2,2048]{2,1,0:T(2,128)(2,1)}), bf16[128,2,2048]{2,1,0:T(2,128)(2,1)S(1)}, u32[]{:S(2)}, u32[]{:S(2)}) async-start(bf16[128,2,2048]{2,1,0:T(2,128)(2,1)} %reshape.141), calls=%async_computation.1 | async-start | bytes 2097152 | tf_op jit(solution)/shard_map/all_to_all | solution.py:52
  57.3 0.0 all-gather.3.cloned.1.call-start
  57.3 31.4 %all-to-all-done.1 = bf16[128,2,2048]{2,1,0:T(2,128)(2,1)S(1)} async-done(((bf16[128,2,2048]{2,1,0:T(2,128)(2,1)}), bf16[128,2,2048]{2,1,0:T(2,128)(2,1)S(1)}, u32[]{:S(2)}, u32[]{:S(2)}) %all-to-all-start.1) | async-done | bytes 1048608 | tf_op jit(solution)/shard_map/all_to_all | solution.py:52
  88.7 0.4 reshape.142
  89.1 1.8 gather_fusion.1
  90.9 0.0 all-gather.3.cloned.1.call-update
  91.0 0.0 all-reduce.4.cloned.1.call-start
  91.0 74.7 %all-gather.3.cloned.1.call-done = bf16[2304,2048]{1,0:T(8,128)(2,1)} async-done(((bf16[144,2048]{1,0:T(8,128)(2,1)}), bf16[2304,2048]{1,0:T(8,128)(2,1)}) %all-gather.3.cloned.1.call-update) | async-done | bytes 9437200 | tf_op jit(solution)/shard_map/all_gather | solution.py:60
  165.8 8.0 %convolution_bitcast_fusion = f32[144,2304]{1,0:T(8,128)} fusion(bf16[2304,2048]{1,0:T(8,128)(2,1)} %all-gather.3.cloned.1.call-done, bf16[144,2048]{1,0:T(8,128)(2,1)S(1)} %copy-done), kind=kOutput, calls=%fused_computation.6 | convolution fusion | flops 1358954496 | bytes 11354112 | tf_op jit(solution)/shard_map/dot_general | solution.py:58
  173.8 0.0 all-reduce.4.cloned.1.call-update
  173.8 0.2 reduce-scatter.2.cloned.1.call-start
  174.1 30.4 %all-reduce.4.cloned.1.call-done = f32[144,2304]{1,0:T(8,128)} async-done(((f32[144,2304]{1,0:T(8,128)}), f32[144,2304]{1,0:T(8,128)}) %all-reduce.4.cloned.1.call-update) | async-done | bytes 1327120 | tf_op jit(solution)/shard_map/psum | solution.py:64
  204.5 1.6 fusion.32
  206.1 0.1 copy-done.2
  206.2 0.4 exponential_reduce_fusion
  206.6 2.8 gather_fusion.2
  209.4 0.6 fusion.24
  210.0 5.3 convolution_convert_fusion
  215.3 93.3 %reduce-scatter.2.cloned.1.call-done = bf16[144,2048]{1,0:T(8,128)(2,1)} async-done(((bf16[2304,2048]{1,0:T(8,128)(2,1)}), bf16[144,2048]{1,0:T(8,128)(2,1)}) %reduce-scatter.2.cloned.1.call-update) | async-done | bytes 589840 | tf_op jit(solution)/shard_map/reduce_scatter | solution.py:74
  308.6 2.3 scatter_custom_fusion.1
  310.9 1.5 reshape.143
  312.4 12.7 %all-to-all-start.2 = ((bf16[128,2,2048]{2,1,0:T(2,128)(2,1)}), bf16[128,2,2048]{2,1,0:T(2,128)(2,1)}, u32[]{:S(2)}, u32[]{:S(2)}) async-start(bf16[128,2,2048]{2,1,0:T(2,128)(2,1)} %reshape.143), calls=%async_computation.3 | async-start | bytes 2097152 | tf_op jit(solution)/shard_map/all_to_all | solution.py:83
  325.2 0.0 all-reduce.6.cloned.1.call-start
  325.2 0.1 eq.60
  325.4 29.3 %all-to-all-done.2 = bf16[128,2,2048]{2,1,0:T(2,128)(2,1)} async-done(((bf16[128,2,2048]{2,1,0:T(2,128)(2,1)}), bf16[128,2,2048]{2,1,0:T(2,128)(2,1)}, u32[]{:S(2)}, u32[]{:S(2)}) %all-to-all-start.2) | async-done | bytes 1048608 | tf_op jit(solution)/shard_map/all_to_all | solution.py:83
  354.7 2.3 reshape.144
  356.9 3.0 multiply_reduce_fusion
  359.9 2.4 psum.38
  362.4 3.9 fusion
  366.3 205.7 %all-reduce.6.cloned.1.call-done = f32[16,2048]{1,0:T(8,128)} async-done(((f32[16,2048]{1,0:T(8,128)}), f32[16,2048]{1,0:T(8,128)}) %all-reduce.6.cloned.1.call-update) | async-done | bytes 131088 | tf_op jit(solution)/shard_map/psum | solution.py:99
  572.0 1.6 copy.19
  (32 shorter events, 0.2 us)
Async XLA Ops:
  7.2 158.6 %copy-start = (bf16[144,2048]{1,0:T(8,128)(2,1)S(1)}, bf16[144,2048]{1,0:T(8,128)(2,1)}, u32[]{:S(2)}) copy-start(bf16[144,2048]{1,0:T(8,128)(2,1)} %param.11) | copy-start | bytes 1769476
  7.2 25.1 %copy-start.3 = (bf16[256,2048]{1,0:T(8,128)(2,1)S(1)}, bf16[256,2048]{1,0:T(8,128)(2,1)}, u32[]{:S(2)}) copy-start(bf16[256,2048]{1,0:T(8,128)(2,1)} %param.7) | copy-start | bytes 3145732
  7.2 25.1 %copy-start.4 = (bf16[16,2048]{1,0:T(8,128)(2,1)S(1)}, bf16[16,2048]{1,0:T(8,128)(2,1)}, u32[]{:S(2)}) copy-start(bf16[16,2048]{1,0:T(8,128)(2,1)} %param.9) | copy-start | bytes 196612
  11.9 27.3 %all-to-all-start = ((s32[128,1,2]{2,1,0:T(1,128)}), s32[128,1,2]{2,1,0:T(1,128)S(1)}, u32[]{:S(2)}, u32[]{:S(2)}) async-start(s32[128,1,2]{2,1,0:T(1,128)} %bitcast.9), calls=%async_computation | async-start | bytes 131072 | tf_op jit(solution)/shard_map/all_to_all | solution.py:50
  27.3 10.0 %copy-start.5 = (f32[2048]{0:T(1024)S(1)}, f32[2048]{0:T(1024)}, u32[]{:S(2)}) copy-start(f32[2048]{0:T(1024)} %param.10) | copy-start | bytes 24580
  43.5 45.2 %all-to-all-start.1 = ((bf16[128,2,2048]{2,1,0:T(2,128)(2,1)}), bf16[128,2,2048]{2,1,0:T(2,128)(2,1)S(1)}, u32[]{:S(2)}, u32[]{:S(2)}) async-start(bf16[128,2,2048]{2,1,0:T(2,128)(2,1)} %reshape.141), calls=%async_computation.1 | async-start | bytes 2097152 | tf_op jit(solution)/shard_map/all_to_all | solution.py:52
  57.3 108.5 %all-gather.3.cloned.1.call-start = ((), (), s32[]{:S(2)}) async-start(), calls=%async_computation.7 | async-start | bytes 10027008 | tf_op jit(solution)/shard_map/all_gather | solution.py:60
  91.0 113.5 %all-reduce.4.cloned.1.call-start = ((), (), s32[]{:S(2)}) async-start(), calls=%async_computation.4 | async-start | bytes 2654208 | tf_op jit(solution)/shard_map/psum | solution.py:64
  173.8 134.8 %reduce-scatter.2.cloned.1.call-start = ((), (), s32[]{:S(2)}) async-start(), calls=%async_computation.5 | async-start | bytes 10027008 | tf_op jit(solution)/shard_map/reduce_scatter | solution.py:74
  204.5 1.7 copy-start.2
  312.4 44.5 %copy-start.1 = (f32[256,2048]{1,0:T(8,128)S(1)}, f32[256,2048]{1,0:T(8,128)}, u32[]{:S(2)}) copy-start(f32[256,2048]{1,0:T(8,128)} %get-tuple-element.8) | copy-start | bytes 6291460
  312.4 42.2 %all-to-all-start.2 = ((bf16[128,2,2048]{2,1,0:T(2,128)(2,1)}), bf16[128,2,2048]{2,1,0:T(2,128)(2,1)}, u32[]{:S(2)}, u32[]{:S(2)}) async-start(bf16[128,2,2048]{2,1,0:T(2,128)(2,1)} %reshape.143), calls=%async_computation.3 | async-start | bytes 2097152 | tf_op jit(solution)/shard_map/all_to_all | solution.py:83
  325.2 246.8 %all-reduce.6.cloned.1.call-start = ((), (), s32[]{:S(2)}) async-start(), calls=%async_computation.6 | async-start | bytes 262144 | tf_op jit(solution)/shard_map/psum | solution.py:99
Sparse Core Ops, SparseCore 0:
  91.1 74.6 all-gather.2
  173.9 30.5 all-reduce.3
  215.4 93.1 reduce-scatter.1
  366.4 205.5 all-reduce.5
where the time goes:
time: 581 us; the launch traced here: 580 us
  waiting for transfers between devices  465 us (80%)
  starting transfers between devices  42.3 us (7%)
  matrix products  24.3 us (4%)
  local copies, waits for them, and re-layouts  18.5 us (3%)
  between operations  14 us (2%)
  blocking collectives  8.25 us (1%)
  other arithmetic  7.91 us (1%)
    psum x1, waiting for transfers between devices, body(): lax.psum(jnp.dot(low_rank_output.T, dpre, precision=lax.Precision.HIGHEST...  206 us
    reduce_scatter x1, waiting for transfers between devices, body(): lax.psum_scatter(lax.dot_general(dscore, user_context_state, (((0,), (0,)...  93.3 us
    all_gather x1, waiting for transfers between devices, body(): lax.all_gather(hist, 'user', axis=0, tiled=True)  74.7 us
    all_to_all x1, waiting for transfers between devices, body(): lax.all_to_all(found, ('item', 'user'), split_axis=0, concat_axis=0, tile...  31.4 us
    psum x1, waiting for transfers between devices, body(): scores = lax.psum(partial_scores, 'mp') / math.sqrt(MODEL_WIDTH)  30.4 us
    all_to_all x1, waiting for transfers between devices, body(): lax.all_to_all(outgoing.reshape(devices, slots, part_width), ('item', 'us...  29.3 us
    all_to_all x1, starting transfers between devices, body(): lax.all_to_all(wanted, ('item', 'user'), split_axis=0, concat_axis=0, til...  15.4 us
    all_to_all x1, starting transfers between devices, body(): lax.all_to_all(found, ('item', 'user'), split_axis=0, concat_axis=0, tile...  13.7 us
  transfers between devices with their start and end apart: 7, of which 6 were waited for; matrix products, arithmetic and copies ran while one was open for 1% of the time, Pallas kernels for 0%

commit v1 on v0

v1 whole, which is shorter than its diff:
```python
import math

import jax
import jax.numpy as jnp
from jax import lax
from jax.sharding import PartitionSpec as P

MODEL_WIDTH = 4096
LEN = 48
EPS = 1e-06
LOWEST = -1e30


def exchange(x, axis):
    return lax.all_to_all(x, axis, split_axis=0, concat_axis=0, tiled=True)


def swap(x):
    return lax.ppermute(x, "mp", [(0, 1), (1, 0)])


def plane_shift(x, step):
    planes = lax.axis_size("item")
    return lax.ppermute(x, "item", [(z, (z + step) % planes) for z in range(planes)])


def body(
    item_last_hidden,
    frozen_down_weight,
    trained_up_weight,
    embedding_norm_gain,
    user_context_state,
    history_owner_device,
    history_item_row,
):
    stored, part_width = item_last_hidden.shape
    count = history_item_row.shape[0]
    planes = lax.axis_size("item")
    users = lax.axis_size("user")
    devices = planes * users
    group = users * count
    slots = 2 * users
    total = planes * slots
    z = lax.axis_index("item")
    me = lax.axis_index("user")

    queries = lax.all_gather(user_context_state, "user", axis=0, tiled=True)

    code = jnp.arange(count, dtype=jnp.int32) * stored + history_item_row
    named = history_owner_device == jnp.arange(devices, dtype=jnp.int32)[None, :]
    first = jnp.min(jnp.where(named, code[:, None], count * stored), axis=0)
    last = jnp.max(jnp.where(named, code[:, None], -1), axis=0)
    wanted = jnp.stack([jnp.where(last < 0, -1, first), jnp.where(last > first, last, -1)], axis=1)
    asked = exchange(wanted, ("item", "user")).reshape(planes, slots)
    asked = lax.dynamic_slice_in_dim(jnp.concatenate([asked, asked]), z, planes, 0).reshape(total)
    asked_row = jnp.where(asked < 0, -1, asked % stored)
    asked_place = jnp.where(asked < 0, -1, asked // stored)

    rows = item_last_hidden[jnp.maximum(asked_row, 0)]
    note = jnp.broadcast_to(asked_place.astype(jnp.bfloat16)[:, None], (total, 128))
    packet = jnp.concatenate([rows, note], axis=1).reshape(planes, slots, part_width + 128)
    arrived = jnp.concatenate(
        [packet[0]] + [plane_shift(packet[d], d) for d in range(1, planes)], axis=0
    )
    hidden = arrived[:, :part_width]
    place = arrived[:, part_width].astype(jnp.int32)
    asker = (jnp.arange(total, dtype=jnp.int32) % slots) // 2
    used = place >= 0
    position = jnp.where(used, asker * count + place, -1)

    low = jnp.dot(hidden, frozen_down_weight, preferred_element_type=jnp.float32)
    low = low + swap(low)
    pre = hidden.astype(jnp.float32) + jnp.dot(
        low, trained_up_weight.astype(jnp.float32), precision=lax.Precision.HIGHEST
    )
    squares = jnp.sum(pre * pre, axis=1, keepdims=True)
    squares = squares + swap(squares)
    rinv = lax.rsqrt(squares / MODEL_WIDTH + EPS)
    hist = (pre * rinv * embedding_norm_gain).astype(jnp.bfloat16)

    partial = lax.dot_general(
        queries, hist, (((1,), (1,)), ((), ())), preferred_element_type=jnp.float32
    )
    scores = (partial + swap(partial)) / math.sqrt(MODEL_WIDTH)
    line = jnp.arange(group, dtype=jnp.int32)
    valid = line % LEN != LEN - 1
    hit = (line[:, None] + 1 == position[None, :]) & valid[:, None]
    scores = jnp.where(used[None, :], scores, LOWEST)
    top = jnp.max(scores, axis=1)
    mass = jnp.sum(jnp.where(used[None, :], jnp.exp(scores - top[:, None]), 0.0), axis=1)
    positive = jnp.sum(jnp.where(hit, scores, 0.0), axis=1)
    stats = jnp.stack([top, mass, positive])
    stats = exchange(jnp.broadcast_to(stats[None], (users, 3, group)), "user")
    peak = jnp.max(stats[:, 0], axis=0)
    lse = peak + jnp.log(jnp.sum(stats[:, 1] * jnp.exp(stats[:, 0] - peak[None]), axis=0))
    loss = jnp.where(valid, lse - jnp.sum(stats[:, 2], axis=0), 0.0)
    pos_loss = lax.dynamic_slice_in_dim(loss, me * count, count, 0)

    dscore = jnp.where(used[None, :], jnp.exp(scores - lse[:, None]), 0.0) - hit.astype(jnp.float32)
    dscore = jnp.where(valid[:, None], dscore, 0.0).astype(jnp.bfloat16)
    hist_grad = lax.dot_general(
        dscore, queries, (((0,), (0,)), ((), ())), preferred_element_type=jnp.float32
    ).astype(jnp.bfloat16)

    outgoing = hist_grad.reshape(planes, slots, part_width)
    returned = jnp.concatenate(
        [outgoing[0]] + [plane_shift(outgoing[d], -d) for d in range(1, planes)], axis=0
    )
    picker = (jnp.arange(stored, dtype=jnp.int32)[:, None] == asked_row[None, :]).astype(
        jnp.bfloat16
    )
    emb_grad = jnp.dot(picker, returned, preferred_element_type=jnp.float32)

    scaled = hist_grad.astype(jnp.float32) * embedding_norm_gain
    inner = jnp.sum(pre * scaled, axis=1, keepdims=True)
    inner = (inner + swap(inner)) / MODEL_WIDTH
    dpre = rinv * scaled - pre * rinv * rinv * rinv * inner
    b_part = jnp.dot(low.T, dpre, precision=lax.Precision.HIGHEST)
    rank = b_part.shape[0]
    share = part_width // users
    b_part = b_part.reshape(rank, users, share).transpose(1, 0, 2)
    b_part = jnp.sum(exchange(b_part, "user"), axis=0)
    b_part = jnp.sum(
        exchange(jnp.broadcast_to(b_part[None], (planes, rank, share)), "item"), axis=0
    )
    b_grad = exchange(jnp.broadcast_to(b_part[None], (users, rank, share)), "user")
    b_grad = b_grad.transpose(1, 0, 2).reshape(rank, part_width)
    return (pos_loss, emb_grad, b_grad)


def solution(mesh):
    placed = (
        P(("item", "user"), "mp"),
        P("mp", None),
        P(None, "mp"),
        P("mp"),
        P(("item", "user"), "mp"),
        P(("item", "user"), None),
        P(("item", "user")),
    )
    return jax.shard_map(
        body,
        mesh=mesh,
        in_specs=placed,
        out_specs=(P(("item", "user")), P(("item", "user"), "mp"), P(None, "mp")),
        check_vma=False,
    )
```

time: 581 us -> 197 us (0.34)
  waiting for transfers between devices: 465 us -> 68.2 us
  starting transfers between devices: 42.3 us -> 60.4 us
  blocking collectives: 8.25 us -> 16.6 us
  matrix products: 24.3 us -> 16.7 us
  local copies, waits for them, and re-layouts: 18.5 us -> 12.2 us
    psum x2 -> x0, waiting for transfers between devices: 236 us -> none  [the longest x1 206 us: body(): lax.psum(jnp.dot(low_rank_output.T, dpre, precision=lax.Precision.HIGHEST...]
    reduce_scatter x1 -> x0, waiting for transfers between devices: 93.3 us -> none  [body(): lax.psum_scatter(lax.dot_general(dscore, user_context_state, (((0,), (0,)...]
    all_gather x1, waiting for transfers between devices: 74.7 us -> 18.7 us  [body(): queries = lax.all_gather(user_context_state, 'user', axis=0, tiled=True)]
    all_to_all x3 -> x4, waiting for transfers between devices: 60.7 us -> 14.7 us  [exchange(): return lax.all_to_all(x, axis, split_axis=0, concat_axis=0, tiled=True)]
    ppermute x0 -> x18, waiting for transfers between devices: none -> 34.1 us  [the longest x14 27.6 us: plane_shift(): lax.ppermute(x, 'item', [(z, (z + step) % planes) for z in range(planes)])]
    ppermute x0 -> x18, starting transfers between devices: none -> 26.3 us  [the longest x14 25.7 us: plane_shift(): lax.ppermute(x, 'item', [(z, (z + step) % planes) for z in range(planes)])]
    all_to_all x0 -> x1, blocking collectives: none -> 16.6 us  [exchange(): return lax.all_to_all(x, axis, split_axis=0, concat_axis=0, tiled=True)]
    psum x3 -> x0, blocking collectives: 8.25 us -> none  [the longest x1 3.37 us: body(): lax.psum(jnp.dot(item_last_hidden, frozen_down_weight, preferred_element_...]
  transfers between devices with their start and end apart: 7 -> 23, of which waited for: 6 -> 12; matrix products, arithmetic and copies ran while one was open for 1% -> 11% of each run, Pallas kernels for 0% -> 0%
where the time goes in v1:
time: 197 us; the launch traced here: 196 us
  waiting for transfers between devices  68.2 us (35%)
  starting transfers between devices  60.4 us (31%)
  matrix products  16.7 us (8%)
  blocking collectives  16.6 us (8%)
  between operations  14.5 us (7%)
  local copies, waits for them, and re-layouts  12.2 us (6%)
  other arithmetic  7.32 us (4%)
    all_to_all x4, starting transfers between devices, exchange(): return lax.all_to_all(x, axis, split_axis=0, concat_axis=0, tiled=True)  34 us
    ppermute x14, waiting for transfers between devices, plane_shift(): lax.ppermute(x, 'item', [(z, (z + step) % planes) for z in range(planes)])  27.6 us
    ppermute x14, starting transfers between devices, plane_shift(): lax.ppermute(x, 'item', [(z, (z + step) % planes) for z in range(planes)])  25.7 us
    all_gather x1, waiting for transfers between devices, body(): queries = lax.all_gather(user_context_state, 'user', axis=0, tiled=True)  18.7 us
    all_to_all x1, blocking collectives, exchange(): return lax.all_to_all(x, axis, split_axis=0, concat_axis=0, tiled=True)  16.6 us
    all_to_all x4, waiting for transfers between devices, exchange(): return lax.all_to_all(x, axis, split_axis=0, concat_axis=0, tiled=True)  14.7 us
    dot_general x1, matrix products, body(): lax.dot_general(queries, hist, (((1,), (1,)), ((), ())), preferred_elemen...  6.9 us
    ppermute x4, waiting for transfers between devices, swap(): return lax.ppermute(x, 'mp', [(0, 1), (1, 0)])  6.47 us
  transfers between devices with their start and end apart: 23, of which 12 were waited for; matrix products, arithmetic and copies ran while one was open for 11% of the time, Pallas kernels for 0%

profile of v1, /device:TPU:2, one launch (start us, length us, event | category | flops | bytes accessed | tf_op | source)
XLA Modules:
  0.0 195.9 jit_solution(13940098067562344575)
XLA Ops:
  7.2 0.7 all-gather.2.cloned.1.call-update
  7.9 0.7 multiply_add_fusion
  8.6 0.8 select_reduce_fusion.3
  9.4 0.7 copy.23
  10.2 15.4 %all-to-all-start = ((s32[128,1,2]{2,1,0:T(1,128)}), s32[128,1,2]{2,1,0:T(1,128)S(1)}, u32[]{:S(2)}, u32[]{:S(2)}) async-start(s32[128,1,2]{2,1,0:T(1,128)} %copy.23), calls=%async_computation | async-start | bytes 131072 | tf_op jit(solution)/shard_map/all_to_all | solution.py:15
  25.6 11.3 %all-to-all-done = s32[128,1,2]{2,1,0:T(1,128)S(1)} async-done(((s32[128,1,2]{2,1,0:T(1,128)}), s32[128,1,2]{2,1,0:T(1,128)S(1)}, u32[]{:S(2)}, u32[]{:S(2)}) %all-to-all-start) | async-done | bytes 1056 | tf_op jit(solution)/shard_map/all_to_all | solution.py:15
  37.4 0.8 reduce.7
  38.5 1.4 gather_fusion
  40.6 0.8 collective-permute-start
  41.4 0.8 collective-permute-start.1
  42.2 1.8 collective-permute-start.2
  44.0 4.0 %collective-permute-start.3 = (bf16[32,2176]{1,0:T(8,128)(2,1)S(1)}, bf16[32,2176]{1,0:T(8,128)(2,1)S(1)}, u32[]{:S(2)}, u32[]{:S(2)}) collective-permute-start(bf16[32,2176]{1,0:T(8,128)(2,1)S(1)} %get-tuple-element.16), channel_id=1, source_target_pairs={{0,128},{32,160},{64,192},{96,224},{128,0},{160,32},{192,64},{224,... | collective-permute-start | bytes 417800 | tf_op jit(solution)/shard_map/ppermute | solution.py:24
  48.0 2.0 %collective-permute-start.4 = (bf16[32,2176]{1,0:T(8,128)(2,1)S(1)}, bf16[32,2176]{1,0:T(8,128)(2,1)S(1)}, u32[]{:S(2)}, u32[]{:S(2)}) collective-permute-start(bf16[32,2176]{1,0:T(8,128)(2,1)S(1)} %get-tuple-element.17), channel_id=1, source_target_pairs={{0,160},{32,192},{64,224},{96,0},{128,32},{160,64},{192,96},{224,1... | collective-permute-start | bytes 417800 | tf_op jit(solution)/shard_map/ppermute | solution.py:24
  50.3 1.3 collective-permute-start.5
  51.6 6.0 %collective-permute-done.1 = bf16[32,2176]{1,0:T(8,128)(2,1)S(1)} collective-permute-done((bf16[32,2176]{1,0:T(8,128)(2,1)S(1)}, bf16[32,2176]{1,0:T(8,128)(2,1)S(1)}, u32[]{:S(2)}, u32[]{:S(2)}) %collective-permute-start.1) | collective-permute-done | bytes 139296 | tf_op jit(solution)/shard_map/ppermute | solution.py:24
  57.6 6.8 %collective-permute-done.2 = bf16[32,2176]{1,0:T(8,128)(2,1)S(1)} collective-permute-done((bf16[32,2176]{1,0:T(8,128)(2,1)S(1)}, bf16[32,2176]{1,0:T(8,128)(2,1)S(1)}, u32[]{:S(2)}, u32[]{:S(2)}) %collective-permute-start.2) | collective-permute-done | bytes 139296 | tf_op jit(solution)/shard_map/ppermute | solution.py:24
  64.5 5.0 %collective-permute-done.5 = bf16[32,2176]{1,0:T(8,128)(2,1)S(1)} collective-permute-done((bf16[32,2176]{1,0:T(8,128)(2,1)S(1)}, bf16[32,2176]{1,0:T(8,128)(2,1)S(1)}, u32[]{:S(2)}, u32[]{:S(2)}) %collective-permute-start.5) | collective-permute-done | bytes 139296 | tf_op jit(solution)/shard_map/ppermute | solution.py:24
  69.6 1.5 collective-permute-done.6
  71.5 1.2 collective-permute-done.7
  72.7 1.3 multiply_reduce_fusion.1
  74.4 1.0 collective-permute-done.8
  75.4 18.7 %all-gather.2.cloned.1.call-done = bf16[2304,2048]{1,0:T(8,128)(2,1)} async-done(((bf16[144,2048]{1,0:T(8,128)(2,1)}), bf16[2304,2048]{1,0:T(8,128)(2,1)}) %all-gather.2.cloned.1.call-update) | async-done | bytes 9437200 | tf_op jit(solution)/shard_map/all_gather | solution.py:47
  94.1 6.9 %convolution_bitcast_fusion = f32[2304,256]{0,1:T(8,128)S(1)} fusion(bf16[2304,2048]{1,0:T(8,128)(2,1)} %all-gather.2.cloned.1.call-done, f32[2048]{0:T(1024)S(1)} %copy-done.10, f32[256]{0:T(256)S(1)} %bitcast.53, f32[256,2048]{1,0:T(8,128)S(1)} %get-tuple-element.34, bf16[256,2176]{1,0:T(8,128)(2,1)} %copy-done.1), kind=kOutput, calls=%fused_computation.1 | convolution fusion | flops 2418540544 | bytes 14951424 | tf_op jit(solution)/shard_map/dot_general | solution.py:81
  101.4 4.3 %collective-permute-done.9 = f32[2304,256]{0,1:T(8,128)S(1)} collective-permute-done((f32[2304,256]{0,1:T(8,128)S(1)}, f32[2304,256]{0,1:T(8,128)S(1)}, u32[]{:S(2)}, u32[]{:S(2)}) %collective-permute-start.9) | collective-permute-done | bytes 2359328 | tf_op jit(solution)/shard_map/ppermute | solution.py:19
  106.2 1.3 select_reduce_fusion.1
  107.6 16.6 %all_to_all.29 = f32[16,3,2304]{2,1,0:T(4,128)S(1)} all-to-all(f32[16,3,2304]{2,1,0:T(4,128)S(1)} %broadcast_in_dim.128), channel_id=1, replica_groups=mesh['item'=8,'user'=16,'mp'=2] {'user'}, dimensions={0} | all-to-all | bytes 884736 | tf_op jit(solution)/shard_map/all_to_all | solution.py:15
  124.2 1.0 slice_reduce_fusion.1
  125.3 3.4 %multiply_reduce_fusion = (f32[256]{0:T(256)S(1)}, bf16[256,2048]{1,0:T(8,128)(2,1)S(1)}) fusion(f32[2048]{0:T(1024)S(1)} %copy-done.10, f32[256,2048]{1,0:T(8,128)S(1)} %get-tuple-element.34, bf16[256,2176]{1,0:T(8,128)(2,1)S(1)} %copy-done.2, bf16[2304,2048]{1,0:T(8,128)(2,1)S(1)} %bitcast.59, f32[2304,256]{0,1:T(8,128)S(1)} %get-tuple-element.10, ...), kind=kOutput, calls=%fused_computation.18 | convolution fusion | flops 2424307456 | bytes 16022016 | tf_op jit(solution)/shard_map/dot_general | solution.py:101
  128.8 0.8 fusion.49
  129.7 3.3 %collective-permute-start.10 = (bf16[32,2048]{1,0:T(8,128)(2,1)}, bf16[32,2048]{1,0:T(8,128)(2,1)}, u32[]{:S(2)}, u32[]{:S(2)}) collective-permute-start(bf16[32,2048]{1,0:T(8,128)(2,1)} %get-tuple-element.25), channel_id=1, source_target_pairs={{0,224},{32,0},{64,32},{96,64},{128,96},{160,128},{192,160},{224,1... | collective-permute-start | bytes 393224 | tf_op jit(solution)/shard_map/ppermute | solution.py:24
  133.0 1.8 fusion.13
  134.8 0.7 copy.46
  135.5 5.0 %all-to-all-start.2 = ((f32[16,16,128]{2,1,0:T(8,128)}), f32[16,16,128]{2,1,0:T(8,128)S(1)}, u32[]{:S(2)}, u32[]{:S(2)}) async-start(f32[16,16,128]{2,1,0:T(8,128)} %bitcast.48), calls=%async_computation.2 | async-start | bytes 262144 | tf_op jit(solution)/shard_map/all_to_all | solution.py:15
  140.5 2.2 %collective-permute-start.11 = (bf16[32,2048]{1,0:T(8,128)(2,1)}, bf16[32,2048]{1,0:T(8,128)(2,1)S(1)}, u32[]{:S(2)}, u32[]{:S(2)}) collective-permute-start(bf16[32,2048]{1,0:T(8,128)(2,1)} %get-tuple-element.24), channel_id=1, source_target_pairs={{0,192},{32,224},{64,0},{96,32},{128,64},{160,96},{192,128},{224,1... | collective-permute-start | bytes 393224 | tf_op jit(solution)/shard_map/ppermute | solution.py:24
  142.7 1.2 collective-permute-start.12
  143.9 3.9 %collective-permute-start.13 = (bf16[32,2048]{1,0:T(8,128)(2,1)}, bf16[32,2048]{1,0:T(8,128)(2,1)S(1)}, u32[]{:S(2)}, u32[]{:S(2)}) collective-permute-start(bf16[32,2048]{1,0:T(8,128)(2,1)} %get-tuple-element.22), channel_id=1, source_target_pairs={{0,128},{32,160},{64,192},{96,224},{128,0},{160,32},{192,64},{224,... | collective-permute-start | bytes 393224 | tf_op jit(solution)/shard_map/ppermute | solution.py:24
  147.8 1.4 dynamic-slice_select_fusion
  149.8 6.3 %all-to-all-start.3 = ((f32[8,16,128]{2,1,0:T(8,128)}), f32[8,16,128]{2,1,0:T(8,128)S(1)}, u32[]{:S(2)}, u32[]{:S(2)}) async-start(f32[8,16,128]{2,1,0:T(8,128)} %broadcast_in_dim.131), calls=%async_computation.3 | async-start | bytes 131072 | tf_op jit(solution)/shard_map/all_to_all | solution.py:15
  156.1 2.9 %collective-permute-start.15 = (bf16[32,2048]{1,0:T(8,128)(2,1)S(1)}, bf16[32,2048]{1,0:T(8,128)(2,1)S(1)}, u32[]{:S(2)}, u32[]{:S(2)}) collective-permute-start(bf16[32,2048]{1,0:T(8,128)(2,1)S(1)} %get-tuple-element.20), channel_id=1, source_target_pairs={{0,64},{32,96},{64,128},{96,160},{128,192},{160,224},{192,0},{224,... | collective-permute-start | bytes 393224 | tf_op jit(solution)/shard_map/ppermute | solution.py:24
  159.1 1.6 constant_dynamic-update-slice_fusion.13
  160.6 1.5 collective-permute-start.16
  164.1 0.7 constant_dynamic-update-slice_fusion.9
  164.7 8.0 %collective-permute-done.15 = bf16[32,2048]{1,0:T(8,128)(2,1)S(1)} collective-permute-done((bf16[32,2048]{1,0:T(8,128)(2,1)S(1)}, bf16[32,2048]{1,0:T(8,128)(2,1)S(1)}, u32[]{:S(2)}, u32[]{:S(2)}) %collective-permute-start.15) | collective-permute-done | bytes 131104 | tf_op jit(solution)/shard_map/ppermute | solution.py:24
  174.1 0.7 broadcast_in_dim.132
  174.8 7.3 %all-to-all-start.4 = ((f32[16,16,128]{2,1,0:T(8,128)}), f32[16,16,128]{2,1,0:T(8,128)S(1)}, u32[]{:S(2)}, u32[]{:S(2)}) async-start(f32[16,16,128]{2,1,0:T(8,128)} %broadcast_in_dim.132), calls=%async_computation.4 | async-start | bytes 262144 | tf_op jit(solution)/shard_map/all_to_all | solution.py:15
  182.0 3.0 %fusion.23 = f32[256,2048]{1,0:T(8,128)} fusion(bf16[256,2048]{1,0:T(8,128)(2,1)} %constant_dynamic-update-slice_fusion.7, s32[256]{0:T(256)S(1)} %copy-done.6), kind=kOutput, calls=%fused_computation.49 | convolution fusion | flops 268500992 | bytes 3146752 | tf_op jit(solution)/shard_map/dot_general | solution.py:112
  185.0 3.4 %all-to-all-done.4 = f32[16,16,128]{2,1,0:T(8,128)S(1)} async-done(((f32[16,16,128]{2,1,0:T(8,128)}), f32[16,16,128]{2,1,0:T(8,128)S(1)}, u32[]{:S(2)}, u32[]{:S(2)}) %all-to-all-start.4) | async-done | bytes 131104 | tf_op jit(solution)/shard_map/all_to_all | solution.py:15
  188.4 0.7 copy_bitcast_fusion.1
  (94 shorter events, 7.8 us)
Async XLA Ops:
  7.2 31.3 %copy-start = (bf16[256,2048]{1,0:T(8,128)(2,1)S(1)}, bf16[256,2048]{1,0:T(8,128)(2,1)}, u32[]{:S(2)}) copy-start(bf16[256,2048]{1,0:T(8,128)(2,1)} %param.7) | copy-start | bytes 3145732
  7.2 86.9 %all-gather.2.cloned.1.call-start = ((), (), s32[]{:S(2)}) async-start(), calls=%async_computation.5 | async-start | bytes 10027008 | tf_op jit(solution)/shard_map/all_gather | solution.py:47
  10.2 26.7 %all-to-all-start = ((s32[128,1,2]{2,1,0:T(1,128)}), s32[128,1,2]{2,1,0:T(1,128)S(1)}, u32[]{:S(2)}, u32[]{:S(2)}) async-start(s32[128,1,2]{2,1,0:T(1,128)} %copy.23), calls=%async_computation | async-start | bytes 131072 | tf_op jit(solution)/shard_map/all_to_all | solution.py:15
  40.5 30.6 %copy-start.9 = (bf16[2048,16]{0,1:T(8,128)(2,1)S(1)}, bf16[2048,16]{0,1:T(8,128)(2,1)}, u32[]{:S(2)}) copy-start(bf16[2048,16]{0,1:T(8,128)(2,1)} %param.8) | copy-start | bytes 196612
  40.6 32.0 %copy-start.3 = (bf16[16,2048]{1,0:T(8,128)(2,1)S(1)}, bf16[16,2048]{1,0:T(8,128)(2,1)}, u32[]{:S(2)}) copy-start(bf16[16,2048]{1,0:T(8,128)(2,1)} %param.9) | copy-start | bytes 196612
  40.6 9.7 %collective-permute-start = (bf16[32,2176]{1,0:T(8,128)(2,1)S(1)}, bf16[32,2176]{1,0:T(8,128)(2,1)S(1)}, u32[]{:S(2)}, u32[]{:S(2)}) collective-permute-start(bf16[32,2176]{1,0:T(8,128)(2,1)S(1)} %get-tuple-element.13), channel_id=1, source_target_pairs={{0,32},{32,64},{64,96},{96,128},{128,160},{160,192},{192,224},{224... | collective-permute-start | bytes 417800 | tf_op jit(solution)/shard_map/ppermute | solution.py:24
  41.4 16.2 %collective-permute-start.1 = (bf16[32,2176]{1,0:T(8,128)(2,1)S(1)}, bf16[32,2176]{1,0:T(8,128)(2,1)S(1)}, u32[]{:S(2)}, u32[]{:S(2)}) collective-permute-start(bf16[32,2176]{1,0:T(8,128)(2,1)S(1)} %get-tuple-element.14), channel_id=1, source_target_pairs={{0,64},{32,96},{64,128},{96,160},{128,192},{160,224},{192,0},{224,... | collective-permute-start | bytes 417800 | tf_op jit(solution)/shard_map/ppermute | solution.py:24
  42.2 22.2 %collective-permute-start.2 = (bf16[32,2176]{1,0:T(8,128)(2,1)S(1)}, bf16[32,2176]{1,0:T(8,128)(2,1)S(1)}, u32[]{:S(2)}, u32[]{:S(2)}) collective-permute-start(bf16[32,2176]{1,0:T(8,128)(2,1)S(1)} %get-tuple-element.15), channel_id=1, source_target_pairs={{0,96},{32,128},{64,160},{96,192},{128,224},{160,0},{192,32},{224,... | collective-permute-start | bytes 417800 | tf_op jit(solution)/shard_map/ppermute | solution.py:24
  44.0 20.5 %collective-permute-start.3 = (bf16[32,2176]{1,0:T(8,128)(2,1)S(1)}, bf16[32,2176]{1,0:T(8,128)(2,1)S(1)}, u32[]{:S(2)}, u32[]{:S(2)}) collective-permute-start(bf16[32,2176]{1,0:T(8,128)(2,1)S(1)} %get-tuple-element.16), channel_id=1, source_target_pairs={{0,128},{32,160},{64,192},{96,224},{128,0},{160,32},{192,64},{224,... | collective-permute-start | bytes 417800 | tf_op jit(solution)/shard_map/ppermute | solution.py:24
  48.0 16.5 %collective-permute-start.4 = (bf16[32,2176]{1,0:T(8,128)(2,1)S(1)}, bf16[32,2176]{1,0:T(8,128)(2,1)S(1)}, u32[]{:S(2)}, u32[]{:S(2)}) collective-permute-start(bf16[32,2176]{1,0:T(8,128)(2,1)S(1)} %get-tuple-element.17), channel_id=1, source_target_pairs={{0,160},{32,192},{64,224},{96,0},{128,32},{160,64},{192,96},{224,1... | collective-permute-start | bytes 417800 | tf_op jit(solution)/shard_map/ppermute | solution.py:24
  50.3 19.2 %collective-permute-start.5 = (bf16[32,2176]{1,0:T(8,128)(2,1)S(1)}, bf16[32,2176]{1,0:T(8,128)(2,1)S(1)}, u32[]{:S(2)}, u32[]{:S(2)}) collective-permute-start(bf16[32,2176]{1,0:T(8,128)(2,1)S(1)} %get-tuple-element.18), channel_id=1, source_target_pairs={{0,192},{32,224},{64,0},{96,32},{128,64},{160,96},{192,128},{224,1... | collective-permute-start | bytes 417800 | tf_op jit(solution)/shard_map/ppermute | solution.py:24
  57.6 13.5 %collective-permute-start.6 = (bf16[32,2176]{1,0:T(8,128)(2,1)S(1)}, bf16[32,2176]{1,0:T(8,128)(2,1)S(1)}, u32[]{:S(2)}, u32[]{:S(2)}) collective-permute-start(bf16[32,2176]{1,0:T(8,128)(2,1)S(1)} %get-tuple-element.11), channel_id=1, source_target_pairs={{0,224},{32,0},{64,32},{96,64},{128,96},{160,128},{192,160},{224,1... | collective-permute-start | bytes 417800 | tf_op jit(solution)/shard_map/ppermute | solution.py:24
  71.1 2.9 %copy-start.1 = (bf16[256,2176]{1,0:T(8,128)(2,1)}, bf16[256,2176]{1,0:T(8,128)(2,1)S(1)}, u32[]{:S(2)}) copy-start(bf16[256,2176]{1,0:T(8,128)(2,1)S(1)} %constant_dynamic-update-slice_fusion) | copy-start | bytes 3342340
  71.1 23.0 %copy-start.10 = (f32[2048]{0:T(1024)S(1)}, f32[2048]{0:T(1024)}, u32[]{:S(2)}) copy-start(f32[2048]{0:T(1024)} %param.10) | copy-start | bytes 24580
  71.5 1.2 collective-permute-start.7
  74.0 1.4 collective-permute-start.8
  75.4 25.7 %copy-start.7 = (f32[256,1]{0,1:T(1,128)}, f32[256,1]{0,1:T(1,128)S(1)}, u32[]{:S(2)}) copy-start(f32[256,1]{0,1:T(1,128)S(1)} %add_rsqrt_fusion) | copy-start | bytes 3076
  94.1 7.1 %copy-start.2 = (bf16[256,2176]{1,0:T(8,128)(2,1)S(1)}, bf16[256,2176]{1,0:T(8,128)(2,1)}, u32[]{:S(2)}) copy-start(bf16[256,2176]{1,0:T(8,128)(2,1)} %copy-done.1) | copy-start | bytes 3342340
  94.1 31.2 %slice-start = ((s8[9437184]{0:T(1024)(128)(4,1)}), s8[4194304]{0:T(1024)(128)(4,1)S(1)}, s32[]{:S(2)}) async-start(s8[9437184]{0:T(1024)(128)(4,1)} %bitcast.58), calls=%async_computation.6 | async-start | bytes 8388608
  94.1 31.2 %slice-start.1 = ((s8[9437184]{0:T(1024)(128)(4,1)}), s8[4194304]{0:T(1024)(128)(4,1)S(1)}, s32[]{:S(2)}) async-start(s8[9437184]{0:T(1024)(128)(4,1)} %bitcast.58), calls=%async_computation.7 | async-start | bytes 8388608
  101.1 4.6 %collective-permute-start.9 = (f32[2304,256]{0,1:T(8,128)S(1)}, f32[2304,256]{0,1:T(8,128)S(1)}, u32[]{:S(2)}, u32[]{:S(2)}) collective-permute-start(f32[2304,256]{0,1:T(8,128)S(1)} %convolution_bitcast_fusion), channel_id=1, source_target_pairs={{0,1},{1,0},{2,3},{3,2},{4,5},{5,4},{6,7},{7,6},{8,9},{9,8},{10,11... | collective-permute-start | bytes 7077896 | tf_op jit(solution)/shard_map/ppermute | solution.py:19
  101.2 24.1 %copy-start.5 = (pred[2304]{0:T(1024)(128)(4,1)}, pred[2304]{0:T(1024)(128)(4,1)S(1)}, u32[]{:S(2)}) copy-start(pred[2304]{0:T(1024)(128)(4,1)S(1)} %fusion.37) | copy-start | bytes 6916
  101.4 23.9 %slice-start.2 = ((s8[9437184]{0:T(1024)(128)(4,1)}), s8[1048576]{0:T(1024)(128)(4,1)S(1)}, s32[]{:S(2)}) async-start(s8[9437184]{0:T(1024)(128)(4,1)} %bitcast.58), calls=%async_computation.8 | async-start | bytes 2097152
  125.3 3.4 %copy-start.4 = (f32[2304]{0:T(1024)}, f32[2304]{0:T(1024)S(1)}, u32[]{:S(2)}) copy-start(f32[2304]{0:T(1024)S(1)} %log_add_fusion) | copy-start | bytes 27652
  128.7 4.3 %copy-start.8 = (f32[256,1]{0,1:T(1,128)S(1)}, f32[256,1]{0,1:T(1,128)}, u32[]{:S(2)}) copy-start(f32[256,1]{0,1:T(1,128)} %copy-done.7) | copy-start | bytes 3076
  128.7 4.3 %copy-start.11 = (f32[2048]{0:T(1024)S(1)}, f32[2048]{0:T(1024)}, u32[]{:S(2)}) copy-start(f32[2048]{0:T(1024)} %param.10) | copy-start | bytes 24580
  128.7 4.3 %collective-permute-start.17 = (f32[256,1]{0,1:T(1,128)S(1)}, f32[256,1]{0,1:T(1,128)S(1)}, u32[]{:S(2)}, u32[]{:S(2)}) collective-permute-start(f32[256,1]{0,1:T(1,128)S(1)} %bitcast.55), channel_id=1, source_target_pairs={{0,1},{1,0},{2,3},{3,2},{4,5},{5,4},{6,7},{7,6},{8,9},{9,8},{10,11... | collective-permute-start | bytes 3080 | tf_op jit(solution)/shard_map/ppermute | solution.py:19
  129.7 26.5 %collective-permute-start.10 = (bf16[32,2048]{1,0:T(8,128)(2,1)}, bf16[32,2048]{1,0:T(8,128)(2,1)}, u32[]{:S(2)}, u32[]{:S(2)}) collective-permute-start(bf16[32,2048]{1,0:T(8,128)(2,1)} %get-tuple-element.25), channel_id=1, source_target_pairs={{0,224},{32,0},{64,32},{96,64},{128,96},{160,128},{192,160},{224,1... | collective-permute-start | bytes 393224 | tf_op jit(solution)/shard_map/ppermute | solution.py:24
  134.8 47.2 %copy-start.6 = (s32[256]{0:T(256)S(1)}, s32[256]{0:T(256)}, u32[]{:S(2)}) copy-start(s32[256]{0:T(256)} %get-tuple-element.29) | copy-start | bytes 3076
  135.5 13.7 %all-to-all-start.2 = ((f32[16,16,128]{2,1,0:T(8,128)}), f32[16,16,128]{2,1,0:T(8,128)S(1)}, u32[]{:S(2)}, u32[]{:S(2)}) async-start(f32[16,16,128]{2,1,0:T(8,128)} %bitcast.48), calls=%async_computation.2 | async-start | bytes 262144 | tf_op jit(solution)/shard_map/all_to_all | solution.py:15
  140.5 20.1 %collective-permute-start.11 = (bf16[32,2048]{1,0:T(8,128)(2,1)}, bf16[32,2048]{1,0:T(8,128)(2,1)S(1)}, u32[]{:S(2)}, u32[]{:S(2)}) collective-permute-start(bf16[32,2048]{1,0:T(8,128)(2,1)} %get-tuple-element.24), channel_id=1, source_target_pairs={{0,192},{32,224},{64,0},{96,32},{128,64},{160,96},{192,128},{224,1... | collective-permute-start | bytes 393224 | tf_op jit(solution)/shard_map/ppermute | solution.py:24
  142.7 20.1 %collective-permute-start.12 = (bf16[32,2048]{1,0:T(8,128)(2,1)}, bf16[32,2048]{1,0:T(8,128)(2,1)S(1)}, u32[]{:S(2)}, u32[]{:S(2)}) collective-permute-start(bf16[32,2048]{1,0:T(8,128)(2,1)} %get-tuple-element.23), channel_id=1, source_target_pairs={{0,160},{32,192},{64,224},{96,0},{128,32},{160,64},{192,96},{224,1... | collective-permute-start | bytes 393224 | tf_op jit(solution)/shard_map/ppermute | solution.py:24
  143.9 19.5 %collective-permute-start.13 = (bf16[32,2048]{1,0:T(8,128)(2,1)}, bf16[32,2048]{1,0:T(8,128)(2,1)S(1)}, u32[]{:S(2)}, u32[]{:S(2)}) collective-permute-start(bf16[32,2048]{1,0:T(8,128)(2,1)} %get-tuple-element.22), channel_id=1, source_target_pairs={{0,128},{32,160},{64,192},{96,224},{128,0},{160,32},{192,64},{224,... | collective-permute-start | bytes 393224 | tf_op jit(solution)/shard_map/ppermute | solution.py:24
  147.8 16.2 %collective-permute-start.14 = (bf16[32,2048]{1,0:T(8,128)(2,1)S(1)}, bf16[32,2048]{1,0:T(8,128)(2,1)S(1)}, u32[]{:S(2)}, u32[]{:S(2)}) collective-permute-start(bf16[32,2048]{1,0:T(8,128)(2,1)S(1)} %get-tuple-element.21), channel_id=1, source_target_pairs={{0,96},{32,128},{64,160},{96,192},{128,224},{160,0},{192,32},{224,... | collective-permute-start | bytes 393224 | tf_op jit(solution)/shard_map/ppermute | solution.py:24
  149.8 24.3 %all-to-all-start.3 = ((f32[8,16,128]{2,1,0:T(8,128)}), f32[8,16,128]{2,1,0:T(8,128)S(1)}, u32[]{:S(2)}, u32[]{:S(2)}) async-start(f32[8,16,128]{2,1,0:T(8,128)} %broadcast_in_dim.131), calls=%async_computation.3 | async-start | bytes 131072 | tf_op jit(solution)/shard_map/all_to_all | solution.py:15
  156.1 16.6 %collective-permute-start.15 = (bf16[32,2048]{1,0:T(8,128)(2,1)S(1)}, bf16[32,2048]{1,0:T(8,128)(2,1)S(1)}, u32[]{:S(2)}, u32[]{:S(2)}) collective-permute-start(bf16[32,2048]{1,0:T(8,128)(2,1)S(1)} %get-tuple-element.20), channel_id=1, source_target_pairs={{0,64},{32,96},{64,128},{96,160},{128,192},{160,224},{192,0},{224,... | collective-permute-start | bytes 393224 | tf_op jit(solution)/shard_map/ppermute | solution.py:24
  160.6 12.8 %collective-permute-start.16 = (bf16[32,2048]{1,0:T(8,128)(2,1)S(1)}, bf16[32,2048]{1,0:T(8,128)(2,1)S(1)}, u32[]{:S(2)}, u32[]{:S(2)}) collective-permute-start(bf16[32,2048]{1,0:T(8,128)(2,1)S(1)} %get-tuple-element.19), channel_id=1, source_target_pairs={{0,32},{32,64},{64,96},{96,128},{128,160},{160,192},{192,224},{224... | collective-permute-start | bytes 393224 | tf_op jit(solution)/shard_map/ppermute | solution.py:24
  174.8 13.7 %all-to-all-start.4 = ((f32[16,16,128]{2,1,0:T(8,128)}), f32[16,16,128]{2,1,0:T(8,128)S(1)}, u32[]{:S(2)}, u32[]{:S(2)}) async-start(f32[16,16,128]{2,1,0:T(8,128)} %broadcast_in_dim.132), calls=%async_computation.4 | async-start | bytes 262144 | tf_op jit(solution)/shard_map/all_to_all | solution.py:15
Sparse Core Ops, SparseCore 0:
  10.5 83.5 all-gather.1

commit v2 on v1

--- a/solution.py
+++ b/solution.py
@@ -3,12 +3,15 @@
 import jax
 import jax.numpy as jnp
 from jax import lax
+from jax.experimental import pallas as pl
+from jax.experimental.pallas import tpu as pltpu
 from jax.sharding import PartitionSpec as P
 
 MODEL_WIDTH = 4096
 LEN = 48
 EPS = 1e-06
 LOWEST = -1e30
+MIB = 1024 * 1024
 
 
 def exchange(x, axis):
@@ -19,9 +22,41 @@
     return lax.ppermute(x, "mp", [(0, 1), (1, 0)])
 
 
-def plane_shift(x, step):
+def turn(x, by):
+    return lax.dynamic_slice_in_dim(jnp.concatenate([x, x[:3]]), by, 4, 0)
+
+
+def from_x(x, step):
+    pairs = [((u // 4 + step) % 4 * 4 + u % 4, u) for u in range(16)]
+    return lax.ppermute(x, "user", pairs)
+
+
+def from_y(x, step):
+    pairs = [(u // 4 * 4 + (u % 4 + step) % 4, u) for u in range(16)]
+    return lax.ppermute(x, "user", pairs)
+
+
+def add_kernel(left_ref, right_ref, *refs):
+    refs[-1][...] = left_ref[...] + right_ref[...]
+
+
+def add_after(left, right, pieces):
+    vmem = pl.BlockSpec(memory_space=pltpu.VMEM)
+    return pl.pallas_call(
+        add_kernel,
+        out_shape=jax.ShapeDtypeStruct(left.shape, left.dtype),
+        in_specs=[vmem, vmem] + [pl.BlockSpec(memory_space=pl.ANY)] * len(pieces),
+        out_specs=vmem,
+        compiler_params=pltpu.CompilerParams(vmem_limit_bytes=4 * MIB),
+        cost_estimate=pl.CostEstimate(
+            flops=left.size, bytes_accessed=12 * left.size, transcendentals=0
+        ),
+    )(left, right, *pieces)
+
+
+def plane_pair(x, mask):
     planes = lax.axis_size("item")
-    return lax.ppermute(x, "item", [(z, (z + step) % planes) for z in range(planes)])
+    return lax.ppermute(x, "item", [(z, z ^ mask) for z in range(planes)])
 
 
 def body(
@@ -41,7 +76,6 @@
     group = users * count
     slots = 2 * users
     total = planes * slots
-    z = lax.axis_index("item")
     me = lax.axis_index("user")
 
     queries = lax.all_gather(user_context_state, "user", axis=0, tiled=True)
@@ -52,16 +86,14 @@
     last = jnp.max(jnp.where(named, code[:, None], -1), axis=0)
     wanted = jnp.stack([jnp.where(last < 0, -1, first), jnp.where(last > first, last, -1)], axis=1)
     asked = exchange(wanted, ("item", "user")).reshape(planes, slots)
-    asked = lax.dynamic_slice_in_dim(jnp.concatenate([asked, asked]), z, planes, 0).reshape(total)
+    asked = asked.reshape(total)
     asked_row = jnp.where(asked < 0, -1, asked % stored)
     asked_place = jnp.where(asked < 0, -1, asked // stored)
 
     rows = item_last_hidden[jnp.maximum(asked_row, 0)]
     note = jnp.broadcast_to(asked_place.astype(jnp.bfloat16)[:, None], (total, 128))
     packet = jnp.concatenate([rows, note], axis=1).reshape(planes, slots, part_width + 128)
-    arrived = jnp.concatenate(
-        [packet[0]] + [plane_shift(packet[d], d) for d in range(1, planes)], axis=0
-    )
+    arrived = exchange(packet, "item").reshape(total, part_width + 128)
     hidden = arrived[:, :part_width]
     place = arrived[:, part_width].astype(jnp.int32)
     asker = (jnp.arange(total, dtype=jnp.int32) % slots) // 2
@@ -78,34 +110,37 @@
     rinv = lax.rsqrt(squares / MODEL_WIDTH + EPS)
     hist = (pre * rinv * embedding_norm_gain).astype(jnp.bfloat16)
 
-    partial = lax.dot_general(
-        queries, hist, (((1,), (1,)), ((), ())), preferred_element_type=jnp.float32
-    )
-    scores = (partial + swap(partial)) / math.sqrt(MODEL_WIDTH)
     line = jnp.arange(group, dtype=jnp.int32)
     valid = line % LEN != LEN - 1
     hit = (line[:, None] + 1 == position[None, :]) & valid[:, None]
-    scores = jnp.where(used[None, :], scores, LOWEST)
+    cut = group // 2
+    hist = lax.optimization_barrier(hist)
+    partials = [
+        lax.dot_general(
+            part, hist, (((1,), (1,)), ((), ())), preferred_element_type=jnp.float32
+        )
+        for part in (queries[:cut], queries[cut:])
+    ]
+    sums = jnp.concatenate([partial + swap(partial) for partial in partials], axis=0)
+    scores = jnp.where(used[None, :], sums / math.sqrt(MODEL_WIDTH), LOWEST)
     top = jnp.max(scores, axis=1)
     mass = jnp.sum(jnp.where(used[None, :], jnp.exp(scores - top[:, None]), 0.0), axis=1)
     positive = jnp.sum(jnp.where(hit, scores, 0.0), axis=1)
-    stats = jnp.stack([top, mass, positive])
-    stats = exchange(jnp.broadcast_to(stats[None], (users, 3, group)), "user")
+    stats = jnp.stack([top, mass])
+    stats = exchange(jnp.broadcast_to(stats[None], (users, 2, group)), "user")
     peak = jnp.max(stats[:, 0], axis=0)
     lse = peak + jnp.log(jnp.sum(stats[:, 1] * jnp.exp(stats[:, 0] - peak[None]), axis=0))
-    loss = jnp.where(valid, lse - jnp.sum(stats[:, 2], axis=0), 0.0)
-    pos_loss = lax.dynamic_slice_in_dim(loss, me * count, count, 0)
 
     dscore = jnp.where(used[None, :], jnp.exp(scores - lse[:, None]), 0.0) - hit.astype(jnp.float32)
     dscore = jnp.where(valid[:, None], dscore, 0.0).astype(jnp.bfloat16)
+    dscore = lax.optimization_barrier(dscore)
     hist_grad = lax.dot_general(
         dscore, queries, (((0,), (0,)), ((), ())), preferred_element_type=jnp.float32
     ).astype(jnp.bfloat16)
+    hist_grad = lax.optimization_barrier(hist_grad)
 
     outgoing = hist_grad.reshape(planes, slots, part_width)
-    returned = jnp.concatenate(
-        [outgoing[0]] + [plane_shift(outgoing[d], -d) for d in range(1, planes)], axis=0
-    )
+    returned = exchange(outgoing, "item").reshape(total, part_width)
     picker = (jnp.arange(stored, dtype=jnp.int32)[:, None] == asked_row[None, :]).astype(
         jnp.bfloat16
     )
@@ -119,10 +154,19 @@
     rank = b_part.shape[0]
     share = part_width // users
     b_part = b_part.reshape(rank, users, share).transpose(1, 0, 2)
-    b_part = jnp.sum(exchange(b_part, "user"), axis=0)
-    b_part = jnp.sum(
-        exchange(jnp.broadcast_to(b_part[None], (planes, rank, share)), "item"), axis=0
-    )
+    positive = jnp.pad(positive.reshape(users, 2, count // 2), ((0, 0), (0, 0), (0, share - count // 2)))
+    both = jnp.concatenate([b_part, positive], axis=1).reshape(4, 4, rank + 2, share)
+    both = turn(both, me // 4)
+    both = both[0] + from_x(both[3], 1) + from_x(both[2], 2) + from_x(both[1], 3)
+    both = turn(both, me % 4)
+    summed = both[0] + from_y(both[3], 1) + from_y(both[2], 2) + from_y(both[1], 3)
+    positive = summed[rank:, : count // 2].reshape(count)
+    own = lax.dynamic_slice_in_dim(lse, me * count, count, 0)
+    pos_loss = jnp.where(valid[:count], own - positive, 0.0)
+    b_part = summed[:rank]
+    for mask in (1, 2):
+        b_part = b_part + plane_pair(b_part, mask)
+    b_part = add_after(b_part, plane_pair(b_part, 4), [returned])
     b_grad = exchange(jnp.broadcast_to(b_part[None], (users, rank, share)), "user")
     b_grad = b_grad.transpose(1, 0, 2).reshape(rank, part_width)
     return (pos_loss, emb_grad, b_grad)

time: 197 us -> 198 us (level)
  blocking collectives: 16.6 us -> 58.1 us
  starting transfers between devices: 60.4 us -> 33.6 us
  waiting for transfers between devices: 68.2 us -> 55 us
  local copies, waits for them, and re-layouts: 12.2 us -> 4.84 us
  matrix products: 16.7 us -> 22.4 us
  other arithmetic: 7.32 us -> 9.5 us
    all_to_all x1 -> x2, blocking collectives: 16.6 us -> 58.1 us  [exchange(): return lax.all_to_all(x, axis, split_axis=0, concat_axis=0, tiled=True)]
    all_to_all x4 -> x3, starting transfers between devices: 34 us -> 18.2 us  [exchange(): return lax.all_to_all(x, axis, split_axis=0, concat_axis=0, tiled=True)]
    ppermute x14 -> x9, starting transfers between devices: 25.7 us -> 14.2 us  [the longest x3 6.8 us: plane_pair(): return lax.ppermute(x, 'item', [(z, z ^ mask) for z in range(planes)])]
    ppermute x14 -> x9, waiting for transfers between devices: 27.6 us -> 19 us  [the longest x3 11.4 us: plane_pair(): return lax.ppermute(x, 'item', [(z, z ^ mask) for z in range(planes)])]
    unnamed x42 -> x12, local copies, waits for them, and re-layouts: 5.04 us -> 0.12 us
    dot_general x1, matrix products: 3.35 us -> 7.55 us  [body(): lax.dot_general(dscore, queries, (((0,), (0,)), ((), ())), preferred_elem...]
    all_to_all x4 -> x3, waiting for transfers between devices: 14.7 us -> 12.3 us  [exchange(): return lax.all_to_all(x, axis, split_axis=0, concat_axis=0, tiled=True)]
    ppermute x4 -> x5, waiting for transfers between devices: 6.47 us -> 4.32 us  [swap(): return lax.ppermute(x, 'mp', [(0, 1), (1, 0)])]
  transfers between devices with their start and end apart: 23 -> 18, of which waited for: 12 -> 13; matrix products, arithmetic and copies ran while one was open for 11% -> 9% of each run, Pallas kernels for 0% -> 0%
where the time goes in v2:
time: 198 us
  blocking collectives  58.1 us (29%)
  waiting for transfers between devices  55 us (28%)
  starting transfers between devices  33.6 us (17%)
  matrix products  22.4 us (11%)
  between operations  14.4 us (7%)
  other arithmetic  9.5 us (5%)
  local copies, waits for them, and re-layouts  4.84 us (2%)
    all_to_all x2, blocking collectives, exchange(): return lax.all_to_all(x, axis, split_axis=0, concat_axis=0, tiled=True)  58.1 us
    all_gather x1, waiting for transfers between devices, body(): queries = lax.all_gather(user_context_state, 'user', axis=0, tiled=True)  18.7 us
    all_to_all x3, starting transfers between devices, exchange(): return lax.all_to_all(x, axis, split_axis=0, concat_axis=0, tiled=True)  18.2 us
    all_to_all x3, waiting for transfers between devices, exchange(): return lax.all_to_all(x, axis, split_axis=0, concat_axis=0, tiled=True)  12.3 us
    ppermute x3, waiting for transfers between devices, plane_pair(): return lax.ppermute(x, 'item', [(z, z ^ mask) for z in range(planes)])  11.4 us
    dot_general x2, matrix products, body(): lax.dot_general(part, hist, (((1,), (1,)), ((), ())), preferred_element_t...  7.79 us
    dot_general x1, matrix products, body(): lax.dot_general(dscore, queries, (((0,), (0,)), ((), ())), preferred_elem...  7.55 us
    ppermute x3, starting transfers between devices, plane_pair(): return lax.ppermute(x, 'item', [(z, z ^ mask) for z in range(planes)])  6.8 us
  transfers between devices with their start and end apart: 18, of which 13 were waited for; matrix products, arithmetic and copies ran while one was open for 9% of the time, Pallas kernels for 0%

profile of v2, /device:TPU:2, one launch (start us, length us, event | category | flops | bytes accessed | tf_op | source)
XLA Modules:
  0.0 197.8 jit_solution(6537176545604566330)
XLA Ops:
  7.2 0.7 all-gather.2.cloned.1.call-update
  7.9 0.7 multiply_add_fusion
  8.6 0.8 select_reduce_fusion.3
  9.5 26.6 %all_to_all.29 = s32[128,1,2]{2,1,0:T(1,128)S(1)} all-to-all(s32[128,1,2]{2,1,0:T(1,128)S(1)} %copy.26), channel_id=1, replica_groups=mesh['item'=8,'user'=16,'mp'=2] {'item','user'}, dimensions={0} | all-to-all | bytes 2048 | tf_op jit(solution)/shard_map/all_to_all | solution.py:18
  36.2 0.5 broadcast.294
  36.8 0.8 reduce.8
  37.8 1.4 gather_fusion
  39.4 31.5 %all_to_all.30 = bf16[8,32,2176]{2,1,0:T(8,128)(2,1)S(1)} all-to-all(bf16[8,32,2176]{2,1,0:T(8,128)(2,1)S(1)} %bitcast.93), channel_id=1, replica_groups=mesh['item'=8,'user'=16,'mp'=2] {'item'}, dimensions={0} | all-to-all | bytes 2228224 | tf_op jit(solution)/shard_map/all_to_all | solution.py:18
  70.9 0.4 fusion.24
  71.3 1.2 collective-permute-done
  72.4 1.3 multiply_reduce_fusion.1
  74.0 1.0 collective-permute-done.1
  75.4 18.7 %all-gather.2.cloned.1.call-done = bf16[2304,2048]{1,0:T(8,128)(2,1)} async-done(((bf16[144,2048]{1,0:T(8,128)(2,1)}), bf16[2304,2048]{1,0:T(8,128)(2,1)}) %all-gather.2.cloned.1.call-update) | async-done | bytes 9437200 | tf_op jit(solution)/shard_map/all_gather | solution.py:81
  94.0 3.9 %fusion.4 = f32[1152,256]{0,1:T(8,128)S(1)} fusion(bf16[256,2048]{1,0:T(8,128)(2,1)S(1)} %multiply_convert_fusion, bf16[2304,2048]{1,0:T(8,128)(2,1)} %all-gather.2.cloned.1.call-done), kind=kOutput, calls=%fused_computation.5 | convolution fusion | flops 1207959552 | bytes 6946816 | tf_op jit(solution)/shard_map/dot_general | solution.py:119
  98.0 3.9 %fusion.7 = f32[1152,256]{0,1:T(8,128)S(1)} fusion(bf16[256,2048]{1,0:T(8,128)(2,1)S(1)} %multiply_convert_fusion, bf16[2304,2048]{1,0:T(8,128)(2,1)} %all-gather.2.cloned.1.call-done), kind=kOutput, calls=%fused_computation.6 | convolution fusion | flops 1207959552 | bytes 6946816 | tf_op jit(solution)/shard_map/dot_general | solution.py:119
  101.9 0.8 collective-permute-start.3
  103.0 2.2 %collective-permute-done.3 = f32[1152,256]{0,1:T(8,128)S(1)} collective-permute-done((f32[1152,256]{0,1:T(8,128)S(1)}, f32[1152,256]{0,1:T(8,128)S(1)}, u32[]{:S(2)}, u32[]{:S(2)}) %collective-permute-start.3) | collective-permute-done | bytes 1179680 | tf_op jit(solution)/shard_map/ppermute | solution.py:22
  105.6 1.2 select_reduce_fusion.1
  106.9 0.8 broadcast_in_dim.126
  107.7 5.7 %all-to-all-start.2 = ((f32[16,2,2304]{2,1,0:T(2,128)}), f32[16,2,2304]{2,1,0:T(2,128)}, u32[]{:S(2)}, u32[]{:S(2)}) async-start(f32[16,2,2304]{2,1,0:T(2,128)} %broadcast_in_dim.126), calls=%async_computation.2 | async-start | bytes 589824 | tf_op jit(solution)/shard_map/all_to_all | solution.py:18
  113.4 7.7 %all-to-all-done.2 = f32[16,2,2304]{2,1,0:T(2,128)} async-done(((f32[16,2,2304]{2,1,0:T(2,128)}), f32[16,2,2304]{2,1,0:T(2,128)}, u32[]{:S(2)}, u32[]{:S(2)}) %all-to-all-start.2) | async-done | bytes 294944 | tf_op jit(solution)/shard_map/all_to_all | solution.py:18
  121.1 1.4 fusion.50
  122.6 1.1 select_convert_fusion
  123.7 7.5 %convolution_convert_fusion = bf16[256,2048]{1,0:T(8,128)(2,1)} fusion(bf16[2304,256]{0,1:T(8,128)(2,1)S(1)} %select_convert_fusion, bf16[2304,2048]{1,0:T(8,128)(2,1)} %all-gather.2.cloned.1.call-done), kind=kOutput, calls=%fused_computation.8 | convolution fusion | flops 2416443392 | bytes 11665408 | tf_op jit(solution)/shard_map/dot_general | solution.py:137
  131.3 1.6 multiply_reduce_fusion
  133.1 7.0 %all-to-all-start.3 = ((bf16[8,32,2048]{2,1,0:T(8,128)(2,1)}), bf16[8,32,2048]{2,1,0:T(8,128)(2,1)S(1)}, u32[]{:S(2)}, u32[]{:S(2)}) async-start(bf16[8,32,2048]{2,1,0:T(8,128)(2,1)} %bitcast.25), calls=%async_computation.3 | async-start | bytes 2097152 | tf_op jit(solution)/shard_map/all_to_all | solution.py:18
  140.1 3.6 %fusion.18 = f32[2,16,8,128]{3,2,1,0:T(8,128)S(1)} fusion(f32[256,16]{0,1:T(8,128)S(1)} %add.148, bf16[256,2048]{1,0:T(8,128)(2,1)} %convolution_convert_fusion, f32[256,2048]{1,0:T(8,128)} %copy-done.1, f32[256]{0:T(256)S(1)} %bitcast.106, f32[2048]{0:T(1024)S(1)} %copy-done.4, f32[256]{0:T(256)S(1)} %bitcast.99), kind=kOutput, calls=%fused_computation.26 | convolution fusion | flops 104857600 | bytes 3303424 | tf_op jit(solution)/shard_map/dot_general | solution.py:153
  143.8 1.9 collective-permute-start.5
  145.8 0.7 collective-permute-start.6
  146.4 1.9 collective-permute-start.7
  148.3 3.1 %collective-permute-done.6 = f32[4,18,128]{2,1,0:T(8,128)S(1)} collective-permute-done((f32[4,18,128]{2,1,0:T(8,128)S(1)}, f32[4,18,128]{2,1,0:T(8,128)S(1)}, u32[]{:S(2)}, u32[]{:S(2)}) %collective-permute-start.6) | collective-permute-done | bytes 36896 | tf_op jit(solution)/shard_map/ppermute | solution.py:31
  151.5 1.0 collective-permute-start.8
  152.5 1.5 collective-permute-start.9
  154.0 0.4 collective-permute-start.10
  154.4 0.8 collective-permute-done.8
  155.2 2.5 %collective-permute-done.9 = f32[18,128]{1,0:T(8,128)S(1)} collective-permute-done((f32[18,128]{1,0:T(8,128)S(1)}, f32[18,128]{1,0:T(8,128)S(1)}, u32[]{:S(2)}, u32[]{:S(2)}) %collective-permute-start.9) | collective-permute-done | bytes 9248 | tf_op jit(solution)/shard_map/ppermute | solution.py:36
  157.7 1.2 collective-permute-done.10
  158.9 2.1 %collective-permute-start.11 = (f32[16,128]{1,0:T(8,128)S(1)}, f32[16,128]{1,0:T(8,128)S(1)}, u32[]{:S(2)}, u32[]{:S(2)}) collective-permute-start(f32[16,128]{1,0:T(8,128)S(1)} %slice.101), channel_id=1, source_target_pairs={{0,32},{32,0},{64,96},{96,64},{128,160},{160,128},{192,224},{224,1... | collective-permute-start | bytes 24584 | tf_op jit(solution)/shard_map/ppermute | solution.py:59
  161.0 4.8 %collective-permute-done.11 = f32[16,128]{1,0:T(8,128)S(1)} collective-permute-done((f32[16,128]{1,0:T(8,128)S(1)}, f32[16,128]{1,0:T(8,128)S(1)}, u32[]{:S(2)}, u32[]{:S(2)}) %collective-permute-start.11) | collective-permute-done | bytes 8224 | tf_op jit(solution)/shard_map/ppermute | solution.py:59
  166.1 4.2 %collective-permute-done.12 = f32[16,128]{1,0:T(8,128)S(1)} collective-permute-done((f32[16,128]{1,0:T(8,128)S(1)}, f32[16,128]{1,0:T(8,128)S(1)}, u32[]{:S(2)}, u32[]{:S(2)}) %collective-permute-start.12) | collective-permute-done | bytes 8224 | tf_op jit(solution)/shard_map/ppermute | solution.py:59
  170.3 4.5 %collective-permute-start.13 = (f32[16,128]{1,0:T(8,128)S(1)}, f32[16,128]{1,0:T(8,128)S(1)}, u32[]{:S(2)}, u32[]{:S(2)}) collective-permute-start(f32[16,128]{1,0:T(8,128)S(1)} %add.173.left_ref), channel_id=1, source_target_pairs={{0,128},{32,160},{64,192},{96,224},{128,0},{160,32},{192,64},{224,... | collective-permute-start | bytes 24584 | tf_op jit(solution)/shard_map/ppermute | solution.py:59
  174.8 0.6 slice_select_fusion
  175.4 2.4 %collective-permute-done.13.right_ref = f32[16,128]{1,0:T(8,128)S(1)} collective-permute-done((f32[16,128]{1,0:T(8,128)S(1)}, f32[16,128]{1,0:T(8,128)S(1)}, u32[]{:S(2)}, u32[]{:S(2)}) %collective-permute-start.13) | collective-permute-done | bytes 8224 | tf_op jit(solution)/shard_map/ppermute | solution.py:59
  177.9 0.7 broadcast_in_dim.130
  178.5 5.4 %all-to-all-start.4 = ((f32[16,16,128]{2,1,0:T(8,128)}), f32[16,16,128]{2,1,0:T(8,128)S(1)}, u32[]{:S(2)}, u32[]{:S(2)}) async-start(f32[16,16,128]{2,1,0:T(8,128)} %broadcast_in_dim.130), calls=%async_computation.4 | async-start | bytes 262144 | tf_op jit(solution)/shard_map/all_to_all | solution.py:18
  183.9 1.8 fusion.26
  185.7 4.6 %all-to-all-done.4 = f32[16,16,128]{2,1,0:T(8,128)S(1)} async-done(((f32[16,16,128]{2,1,0:T(8,128)}), f32[16,16,128]{2,1,0:T(8,128)S(1)}, u32[]{:S(2)}, u32[]{:S(2)}) %all-to-all-start.4) | async-done | bytes 131104 | tf_op jit(solution)/shard_map/all_to_all | solution.py:18
  190.3 0.7 copy_bitcast_fusion.1
  (67 shorter events, 2.8 us)
Async XLA Ops:
  7.2 30.6 %copy-start = (bf16[256,2048]{1,0:T(8,128)(2,1)S(1)}, bf16[256,2048]{1,0:T(8,128)(2,1)}, u32[]{:S(2)}) copy-start(bf16[256,2048]{1,0:T(8,128)(2,1)} %param.7) | copy-start | bytes 3145732
  7.2 86.9 %all-gather.2.cloned.1.call-start = ((), (), s32[]{:S(2)}) async-start(), calls=%async_computation.5 | async-start | bytes 10027008 | tf_op jit(solution)/shard_map/all_gather | solution.py:81
  39.2 31.6 %copy-start.5 = (bf16[2048,16]{0,1:T(8,128)(2,1)S(1)}, bf16[2048,16]{0,1:T(8,128)(2,1)}, u32[]{:S(2)}) copy-start(bf16[2048,16]{0,1:T(8,128)(2,1)} %param.8) | copy-start | bytes 196612
  39.4 33.1 %copy-start.3 = (bf16[16,2048]{1,0:T(8,128)(2,1)S(1)}, bf16[16,2048]{1,0:T(8,128)(2,1)}, u32[]{:S(2)}) copy-start(bf16[16,2048]{1,0:T(8,128)(2,1)} %param.9) | copy-start | bytes 196612
  70.9 4.2 %copy-start.4 = (f32[2048]{0:T(1024)S(1)}, f32[2048]{0:T(1024)}, u32[]{:S(2)}) copy-start(f32[2048]{0:T(1024)} %param.10) | copy-start | bytes 24580
  71.2 1.2 collective-permute-start
  73.8 1.3 copy-start.1
  73.8 1.2 collective-permute-start.1
  97.9 4.9 %collective-permute-start.2 = (f32[1152,256]{0,1:T(8,128)S(1)}, f32[1152,256]{0,1:T(8,128)S(1)}, u32[]{:S(2)}, u32[]{:S(2)}) collective-permute-start(f32[1152,256]{0,1:T(8,128)S(1)} %fusion.4), channel_id=1, source_target_pairs={{0,1},{1,0},{2,3},{3,2},{4,5},{5,4},{6,7},{7,6},{8,9},{9,8},{10,11... | collective-permute-start | bytes 3538952 | tf_op jit(solution)/shard_map/ppermute | solution.py:22
  101.9 3.2 %collective-permute-start.3 = (f32[1152,256]{0,1:T(8,128)S(1)}, f32[1152,256]{0,1:T(8,128)S(1)}, u32[]{:S(2)}, u32[]{:S(2)}) collective-permute-start(f32[1152,256]{0,1:T(8,128)S(1)} %fusion.7), channel_id=1, source_target_pairs={{0,1},{1,0},{2,3},{3,2},{4,5},{5,4},{6,7},{7,6},{8,9},{9,8},{10,11... | collective-permute-start | bytes 3538952 | tf_op jit(solution)/shard_map/ppermute | solution.py:22
  107.7 13.4 %all-to-all-start.2 = ((f32[16,2,2304]{2,1,0:T(2,128)}), f32[16,2,2304]{2,1,0:T(2,128)}, u32[]{:S(2)}, u32[]{:S(2)}) async-start(f32[16,2,2304]{2,1,0:T(2,128)} %broadcast_in_dim.126), calls=%async_computation.2 | async-start | bytes 589824 | tf_op jit(solution)/shard_map/all_to_all | solution.py:18
  123.7 7.6 %copy-start.2 = (f32[256,2048]{1,0:T(8,128)S(1)}, f32[256,2048]{1,0:T(8,128)}, u32[]{:S(2)}) copy-start(f32[256,2048]{1,0:T(8,128)} %copy-done.1) | copy-start | bytes 6291460
  132.9 7.2 %collective-permute-start.4 = (f32[256,1]{0,1:T(1,128)S(1)}, f32[256,1]{0,1:T(1,128)S(1)}, u32[]{:S(2)}, u32[]{:S(2)}) collective-permute-start(f32[256,1]{0,1:T(1,128)S(1)} %bitcast.100), channel_id=1, source_target_pairs={{0,1},{1,0},{2,3},{3,2},{4,5},{5,4},{6,7},{7,6},{8,9},{9,8},{10,11... | collective-permute-start | bytes 3080 | tf_op jit(solution)/shard_map/ppermute | solution.py:22
  133.1 44.8 %all-to-all-start.3 = ((bf16[8,32,2048]{2,1,0:T(8,128)(2,1)}), bf16[8,32,2048]{2,1,0:T(8,128)(2,1)S(1)}, u32[]{:S(2)}, u32[]{:S(2)}) async-start(bf16[8,32,2048]{2,1,0:T(8,128)(2,1)} %bitcast.25), calls=%async_computation.3 | async-start | bytes 2097152 | tf_op jit(solution)/shard_map/all_to_all | solution.py:18
  143.8 4.5 %collective-permute-start.5 = (f32[4,18,128]{2,1,0:T(8,128)S(1)}, f32[4,18,128]{2,1,0:T(8,128)S(1)}, u32[]{:S(2)}, u32[]{:S(2)}) collective-permute-start(f32[4,18,128]{2,1,0:T(8,128)S(1)} %get-tuple-element.10), channel_id=1, source_target_pairs={{8,0},{10,2},{12,4},{14,6},{16,8},{18,10},{20,12},{22,14},{24,16},... | collective-permute-start | bytes 110600 | tf_op jit(solution)/shard_map/ppermute | solution.py:31
  145.8 5.6 %collective-permute-start.6 = (f32[4,18,128]{2,1,0:T(8,128)S(1)}, f32[4,18,128]{2,1,0:T(8,128)S(1)}, u32[]{:S(2)}, u32[]{:S(2)}) collective-permute-start(f32[4,18,128]{2,1,0:T(8,128)S(1)} %get-tuple-element.11), channel_id=1, source_target_pairs={{16,0},{18,2},{20,4},{22,6},{24,8},{26,10},{28,12},{30,14},{0,16},... | collective-permute-start | bytes 110600 | tf_op jit(solution)/shard_map/ppermute | solution.py:31
  146.4 4.9 %collective-permute-start.7 = (f32[4,18,128]{2,1,0:T(8,128)S(1)}, f32[4,18,128]{2,1,0:T(8,128)S(1)}, u32[]{:S(2)}, u32[]{:S(2)}) collective-permute-start(f32[4,18,128]{2,1,0:T(8,128)S(1)} %get-tuple-element.12), channel_id=1, source_target_pairs={{24,0},{26,2},{28,4},{30,6},{0,8},{2,10},{4,12},{6,14},{8,16},{10,... | collective-permute-start | bytes 110600 | tf_op jit(solution)/shard_map/ppermute | solution.py:31
  151.5 3.8 %collective-permute-start.8 = (f32[18,128]{1,0:T(8,128)S(1)}, f32[18,128]{1,0:T(8,128)S(1)}, u32[]{:S(2)}, u32[]{:S(2)}) collective-permute-start(f32[18,128]{1,0:T(8,128)S(1)} %get-tuple-element.13), channel_id=1, source_target_pairs={{2,0},{4,2},{6,4},{0,6},{10,8},{12,10},{14,12},{8,14},{18,16},{20,... | collective-permute-start | bytes 27656 | tf_op jit(solution)/shard_map/ppermute | solution.py:36
  152.5 5.2 %collective-permute-start.9 = (f32[18,128]{1,0:T(8,128)S(1)}, f32[18,128]{1,0:T(8,128)S(1)}, u32[]{:S(2)}, u32[]{:S(2)}) collective-permute-start(f32[18,128]{1,0:T(8,128)S(1)} %get-tuple-element.14), channel_id=1, source_target_pairs={{4,0},{6,2},{0,4},{2,6},{12,8},{14,10},{8,12},{10,14},{20,16},{22,... | collective-permute-start | bytes 27656 | tf_op jit(solution)/shard_map/ppermute | solution.py:36
  154.0 4.9 %collective-permute-start.10 = (f32[18,128]{1,0:T(8,128)S(1)}, f32[18,128]{1,0:T(8,128)S(1)}, u32[]{:S(2)}, u32[]{:S(2)}) collective-permute-start(f32[18,128]{1,0:T(8,128)S(1)} %get-tuple-element.15), channel_id=1, source_target_pairs={{6,0},{0,2},{2,4},{4,6},{14,8},{8,10},{10,12},{12,14},{22,16},{16,... | collective-permute-start | bytes 27656 | tf_op jit(solution)/shard_map/ppermute | solution.py:36
  158.9 6.8 %collective-permute-start.11 = (f32[16,128]{1,0:T(8,128)S(1)}, f32[16,128]{1,0:T(8,128)S(1)}, u32[]{:S(2)}, u32[]{:S(2)}) collective-permute-start(f32[16,128]{1,0:T(8,128)S(1)} %slice.101), channel_id=1, source_target_pairs={{0,32},{32,0},{64,96},{96,64},{128,160},{160,128},{192,224},{224,1... | collective-permute-start | bytes 24584 | tf_op jit(solution)/shard_map/ppermute | solution.py:59
  165.7 4.5 %collective-permute-start.12 = (f32[16,128]{1,0:T(8,128)S(1)}, f32[16,128]{1,0:T(8,128)S(1)}, u32[]{:S(2)}, u32[]{:S(2)}) collective-permute-start(f32[16,128]{1,0:T(8,128)S(1)} %slice_add_fusion), channel_id=1, source_target_pairs={{0,64},{32,96},{64,0},{96,32},{128,192},{160,224},{192,128},{224,1... | collective-permute-start | bytes 24584 | tf_op jit(solution)/shard_map/ppermute | solution.py:59
  170.3 7.6 %collective-permute-start.13 = (f32[16,128]{1,0:T(8,128)S(1)}, f32[16,128]{1,0:T(8,128)S(1)}, u32[]{:S(2)}, u32[]{:S(2)}) collective-permute-start(f32[16,128]{1,0:T(8,128)S(1)} %add.173.left_ref), channel_id=1, source_target_pairs={{0,128},{32,160},{64,192},{96,224},{128,0},{160,32},{192,64},{224,... | collective-permute-start | bytes 24584 | tf_op jit(solution)/shard_map/ppermute | solution.py:59
  178.5 11.8 %all-to-all-start.4 = ((f32[16,16,128]{2,1,0:T(8,128)}), f32[16,16,128]{2,1,0:T(8,128)S(1)}, u32[]{:S(2)}, u32[]{:S(2)}) async-start(f32[16,16,128]{2,1,0:T(8,128)} %broadcast_in_dim.130), calls=%async_computation.4 | async-start | bytes 262144 | tf_op jit(solution)/shard_map/all_to_all | solution.py:18
Sparse Core Ops, SparseCore 0:
  10.5 83.5 all-gather.1

commit v3 on v2

--- a/solution.py
+++ b/solution.py
@@ -87,7 +87,8 @@
     wanted = jnp.stack([jnp.where(last < 0, -1, first), jnp.where(last > first, last, -1)], axis=1)
     asked = exchange(wanted, ("item", "user")).reshape(planes, slots)
     asked = asked.reshape(total)
-    asked_row = jnp.where(asked < 0, -1, asked % stored)
+    my_x, my_y = me // 4, me % 4
+    asked_row = jnp.where(asked < 0, -1 - my_x - my_y, asked % stored)
     asked_place = jnp.where(asked < 0, -1, asked // stored)
 
     rows = item_last_hidden[jnp.maximum(asked_row, 0)]
@@ -114,7 +115,6 @@
     valid = line % LEN != LEN - 1
     hit = (line[:, None] + 1 == position[None, :]) & valid[:, None]
     cut = group // 2
-    hist = lax.optimization_barrier(hist)
     partials = [
         lax.dot_general(
             part, hist, (((1,), (1,)), ((), ())), preferred_element_type=jnp.float32
@@ -131,13 +131,12 @@
     peak = jnp.max(stats[:, 0], axis=0)
     lse = peak + jnp.log(jnp.sum(stats[:, 1] * jnp.exp(stats[:, 0] - peak[None]), axis=0))
 
+    positive = jnp.where(lse > LOWEST, positive, 0.0)
     dscore = jnp.where(used[None, :], jnp.exp(scores - lse[:, None]), 0.0) - hit.astype(jnp.float32)
     dscore = jnp.where(valid[:, None], dscore, 0.0).astype(jnp.bfloat16)
-    dscore = lax.optimization_barrier(dscore)
     hist_grad = lax.dot_general(
         dscore, queries, (((0,), (0,)), ((), ())), preferred_element_type=jnp.float32
     ).astype(jnp.bfloat16)
-    hist_grad = lax.optimization_barrier(hist_grad)
 
     outgoing = hist_grad.reshape(planes, slots, part_width)
     returned = exchange(outgoing, "item").reshape(total, part_width)
@@ -156,19 +155,20 @@
     b_part = b_part.reshape(rank, users, share).transpose(1, 0, 2)
     positive = jnp.pad(positive.reshape(users, 2, count // 2), ((0, 0), (0, 0), (0, share - count // 2)))
     both = jnp.concatenate([b_part, positive], axis=1).reshape(4, 4, rank + 2, share)
-    both = turn(both, me // 4)
+    both = turn(both, my_x)
     both = both[0] + from_x(both[3], 1) + from_x(both[2], 2) + from_x(both[1], 3)
-    both = turn(both, me % 4)
-    summed = both[0] + from_y(both[3], 1) + from_y(both[2], 2) + from_y(both[1], 3)
+    both = (both + from_y(both, 2)) + (from_y(both, 1) + from_y(both, 3))
+    summed = lax.dynamic_index_in_dim(both, my_y, 0, keepdims=False)
     positive = summed[rank:, : count // 2].reshape(count)
     own = lax.dynamic_slice_in_dim(lse, me * count, count, 0)
     pos_loss = jnp.where(valid[:count], own - positive, 0.0)
-    b_part = summed[:rank]
+    b_part = both[:, :rank]
     for mask in (1, 2):
         b_part = b_part + plane_pair(b_part, mask)
     b_part = add_after(b_part, plane_pair(b_part, 4), [returned])
-    b_grad = exchange(jnp.broadcast_to(b_part[None], (users, rank, share)), "user")
-    b_grad = b_grad.transpose(1, 0, 2).reshape(rank, part_width)
+    b_grad = jnp.stack([b_part] + [from_x(b_part, step) for step in (1, 2, 3)])
+    b_grad = turn(b_grad, (4 - my_x) % 4)
+    b_grad = b_grad.transpose(2, 0, 1, 3).reshape(rank, part_width)
     return (pos_loss, emb_grad, b_grad)
 
 

time: 198 us -> 188 us (0.949)
  blocking collectives: 58.1 us -> 44.6 us
  starting transfers between devices: 33.6 us -> 44.4 us
  other arithmetic: 9.5 us -> 5.42 us
  waiting for transfers between devices: 55 us -> 53 us
    all_to_all x2, blocking collectives: 58.1 us -> 44.6 us  [exchange(): return lax.all_to_all(x, axis, split_axis=0, concat_axis=0, tiled=True)]
    ppermute x3 -> x6, starting transfers between devices: 4.46 us -> 9.01 us  [from_x(): return lax.ppermute(x, 'user', pairs)]
    all_to_all x3 -> x2, starting transfers between devices: 18.2 us -> 22.5 us  [exchange(): return lax.all_to_all(x, axis, split_axis=0, concat_axis=0, tiled=True)]
    dot_general x1, matrix products: 7.55 us -> 4.28 us  [body(): lax.dot_general(dscore, queries, (((0,), (0,)), ((), ())), preferred_elem...]
    ppermute x3 -> x6, waiting for transfers between devices: 3.08 us -> 4.66 us  [from_x(): return lax.ppermute(x, 'user', pairs)]
    all_to_all x3 -> x2, waiting for transfers between devices: 12.3 us -> 11.3 us  [exchange(): return lax.all_to_all(x, axis, split_axis=0, concat_axis=0, tiled=True)]
  transfers between devices with their start and end apart: 18 -> 20, of which waited for: 13 -> 12; matrix products, arithmetic and copies ran while one was open for 9% -> 10% of each run, Pallas kernels for 0% -> 0%
where the time goes in v3:
time: 188 us; the launch traced here: 187 us
  waiting for transfers between devices  53 us (28%)
  blocking collectives  44.6 us (24%)
  starting transfers between devices  44.4 us (24%)
  matrix products  21.4 us (11%)
  between operations  14.5 us (8%)
  other arithmetic  5.42 us (3%)
  local copies, waits for them, and re-layouts  4.16 us (2%)
    all_to_all x2, blocking collectives, exchange(): return lax.all_to_all(x, axis, split_axis=0, concat_axis=0, tiled=True)  44.6 us
    all_to_all x2, starting transfers between devices, exchange(): return lax.all_to_all(x, axis, split_axis=0, concat_axis=0, tiled=True)  22.5 us
    all_gather x1, waiting for transfers between devices, body(): queries = lax.all_gather(user_context_state, 'user', axis=0, tiled=True)  17.2 us
    all_to_all x2, waiting for transfers between devices, exchange(): return lax.all_to_all(x, axis, split_axis=0, concat_axis=0, tiled=True)  11.3 us
    ppermute x3, waiting for transfers between devices, plane_pair(): return lax.ppermute(x, 'item', [(z, z ^ mask) for z in range(planes)])  9.54 us
    ppermute x6, starting transfers between devices, from_x(): return lax.ppermute(x, 'user', pairs)  9.01 us
    dot_general x2, matrix products, body(): lax.dot_general(part, hist, (((1,), (1,)), ((), ())), preferred_element_t...  8.8 us
    ppermute x3, starting transfers between devices, plane_pair(): return lax.ppermute(x, 'item', [(z, z ^ mask) for z in range(planes)])  8.33 us
  transfers between devices with their start and end apart: 20, of which 12 were waited for; matrix products, arithmetic and copies ran while one was open for 10% of the time, Pallas kernels for 0%

profile of v3, /device:TPU:2, one launch (start us, length us, event | category | flops | bytes accessed | tf_op | source)
XLA Modules:
  0.0 187.5 jit_solution(789637032522688832)
XLA Ops:
  7.2 0.7 all-gather.2.cloned.1.call-update
  7.9 0.7 multiply_add_fusion
  8.6 0.8 select_reduce_fusion.3
  9.4 0.7 copy.24
  10.2 15.4 %all-to-all-start = ((s32[128,1,2]{2,1,0:T(1,128)}), s32[128,1,2]{2,1,0:T(1,128)S(1)}, u32[]{:S(2)}, u32[]{:S(2)}) async-start(s32[128,1,2]{2,1,0:T(1,128)} %copy.24), calls=%async_computation | async-start | bytes 131072 | tf_op jit(solution)/shard_map/all_to_all | solution.py:18
  25.6 11.3 %all-to-all-done = s32[128,1,2]{2,1,0:T(1,128)S(1)} async-done(((s32[128,1,2]{2,1,0:T(1,128)}), s32[128,1,2]{2,1,0:T(1,128)S(1)}, u32[]{:S(2)}, u32[]{:S(2)}) %all-to-all-start) | async-done | bytes 1056 | tf_op jit(solution)/shard_map/all_to_all | solution.py:18
  37.0 0.5 broadcast.300
  37.5 0.8 reduce.8
  38.5 1.4 gather_fusion
  40.1 31.5 %all_to_all.24 = bf16[8,32,2176]{2,1,0:T(8,128)(2,1)S(1)} all-to-all(bf16[8,32,2176]{2,1,0:T(8,128)(2,1)S(1)} %bitcast.85), channel_id=1, replica_groups=mesh['item'=8,'user'=16,'mp'=2] {'item'}, dimensions={0} | all-to-all | bytes 2228224 | tf_op jit(solution)/shard_map/all_to_all | solution.py:18
  71.6 0.4 fusion.30
  72.0 1.2 collective-permute-done
  73.2 2.6 %multiply_reduce_fusion.1 = (f32[256]{0:T(256)S(1)}, f32[256,2048]{1,0:T(8,128)}) fusion(f32[256,16]{0,1:T(8,128)S(1)} %add.158, bf16[16,2048]{1,0:T(8,128)(2,1)S(1)} %copy-done.2, bf16[256,2176]{1,0:T(8,128)(2,1)S(1)} %bitcast.83), kind=kOutput, calls=%fused_computation.24 | convolution fusion | flops 102760192 | bytes 3228672 | tf_op jit(solution)/shard_map/dot_general | solution.py:106
  75.9 1.0 collective-permute-done.1
  76.9 17.2 %all-gather.2.cloned.1.call-done = bf16[2304,2048]{1,0:T(8,128)(2,1)} async-done(((bf16[144,2048]{1,0:T(8,128)(2,1)}), bf16[2304,2048]{1,0:T(8,128)(2,1)}) %all-gather.2.cloned.1.call-update) | async-done | bytes 9437200 | tf_op jit(solution)/shard_map/all_gather | solution.py:81
  94.1 4.7 %fusion.4 = f32[1152,256]{0,1:T(8,128)S(1)} fusion(bf16[2304,2048]{1,0:T(8,128)(2,1)} %all-gather.2.cloned.1.call-done, f32[256,2048]{1,0:T(8,128)} %get-tuple-element.20, f32[2048]{0:T(1024)S(1)} %copy-done.4, f32[256]{0:T(256)S(1)} %bitcast.94), kind=kOutput, calls=%fused_computation.5 | convolution fusion | flops 1209532416 | bytes 8004608 | tf_op jit(solution)/shard_map/dot_general | solution.py:119
  99.0 4.1 %fusion.7 = f32[1152,256]{0,1:T(8,128)S(1)} fusion(bf16[2304,2048]{1,0:T(8,128)(2,1)} %all-gather.2.cloned.1.call-done, f32[256,2048]{1,0:T(8,128)S(1)} %copy-done.1, f32[2048]{0:T(1024)S(1)} %copy-done.4, f32[256]{0:T(256)S(1)} %bitcast.95), kind=kOutput, calls=%fused_computation.6 | convolution fusion | flops 1209532416 | bytes 8004608 | tf_op jit(solution)/shard_map/dot_general | solution.py:119
  103.1 0.7 collective-permute-start.3
  104.1 2.1 %collective-permute-done.3 = f32[1152,256]{0,1:T(8,128)S(1)} collective-permute-done((f32[1152,256]{0,1:T(8,128)S(1)}, f32[1152,256]{0,1:T(8,128)S(1)}, u32[]{:S(2)}, u32[]{:S(2)}) %collective-permute-start.3) | collective-permute-done | bytes 1179680 | tf_op jit(solution)/shard_map/ppermute | solution.py:22
  106.4 0.3 fusion.53
  106.7 1.2 select_reduce_fusion.1
  108.1 13.1 %all_to_all.25 = f32[16,2,2304]{2,1,0:T(2,128)S(1)} all-to-all(f32[16,2,2304]{2,1,0:T(2,128)S(1)} %broadcast_in_dim.127), channel_id=1, replica_groups=mesh['item'=8,'user'=16,'mp'=2] {'user'}, dimensions={0} | all-to-all | bytes 589824 | tf_op jit(solution)/shard_map/all_to_all | solution.py:18
  121.2 0.3 fusion.54
  121.6 4.3 %multiply_reduce_fusion = (f32[256]{0:T(256)S(1)}, bf16[256,2048]{1,0:T(8,128)(2,1)}) fusion(f32[256,2048]{1,0:T(8,128)S(1)} %copy-done.1, f32[2048]{0:T(1024)S(1)} %copy-done.4, bf16[2304,2048]{1,0:T(8,128)(2,1)S(1)} %bitcast.101, s32[2304]{0:T(1024)S(1)} %iota_add_fusion, f32[2304]{0:T(1024)S(1)} %get-tuple-element.8, s32[256]{0:T(256)S(1)} %add_select_fusion.1, ...), kind=kOutput, calls=%fused_computation.18 | convolution fusion | flops 2425028352 | bytes 14973440 | tf_op jit(solution)/shard_map/dot_general | solution.py:137
  126.0 7.0 %all-to-all-start.3 = ((bf16[8,32,2048]{2,1,0:T(8,128)(2,1)}), bf16[8,32,2048]{2,1,0:T(8,128)(2,1)S(1)}, u32[]{:S(2)}, u32[]{:S(2)}) async-start(bf16[8,32,2048]{2,1,0:T(8,128)(2,1)} %bitcast.22), calls=%async_computation.3 | async-start | bytes 2097152 | tf_op jit(solution)/shard_map/all_to_all | solution.py:18
  133.0 3.6 %fusion.24 = f32[2,16,8,128]{3,2,1,0:T(8,128)S(1)} fusion(f32[256,16]{0,1:T(8,128)S(1)} %add.158, bf16[256,2048]{1,0:T(8,128)(2,1)} %get-tuple-element.22, f32[256,2048]{1,0:T(8,128)} %get-tuple-element.20, f32[256]{0:T(256)S(1)} %bitcast.99, f32[2048]{0:T(1024)S(1)} %copy-done.4, f32[256]{0:T(256)S(1)} %bitcast.96), kind=kOutput, calls=%fused_computation.32 | convolution fusion | flops 104857600 | bytes 3303424 | tf_op jit(solution)/shard_map/dot_general | solution.py:152
  136.7 1.9 %collective-permute-start.5 = (f32[4,18,128]{2,1,0:T(8,128)S(1)}, f32[4,18,128]{2,1,0:T(8,128)S(1)}, u32[]{:S(2)}, u32[]{:S(2)}) collective-permute-start(f32[4,18,128]{2,1,0:T(8,128)S(1)} %get-tuple-element.12), channel_id=1, source_target_pairs={{8,0},{10,2},{12,4},{14,6},{16,8},{18,10},{20,12},{22,14},{24,16},... | collective-permute-start | bytes 110600 | tf_op jit(solution)/shard_map/ppermute | solution.py:31
  138.7 0.7 collective-permute-start.6
  139.3 1.9 collective-permute-start.7
  141.2 3.1 %collective-permute-done.6 = f32[4,18,128]{2,1,0:T(8,128)S(1)} collective-permute-done((f32[4,18,128]{2,1,0:T(8,128)S(1)}, f32[4,18,128]{2,1,0:T(8,128)S(1)}, u32[]{:S(2)}, u32[]{:S(2)}) %collective-permute-start.6) | collective-permute-done | bytes 36896 | tf_op jit(solution)/shard_map/ppermute | solution.py:31
  144.3 0.4 collective-permute-start.10
  144.7 2.9 %collective-permute-start.9 = (f32[4,18,128]{2,1,0:T(8,128)S(1)}, f32[4,18,128]{2,1,0:T(8,128)S(1)}, u32[]{:S(2)}, u32[]{:S(2)}) collective-permute-start(f32[4,18,128]{2,1,0:T(8,128)S(1)} %fusion.41), channel_id=1, source_target_pairs={{2,0},{4,2},{6,4},{0,6},{10,8},{12,10},{14,12},{8,14},{18,16},{20,... | collective-permute-start | bytes 110600 | tf_op jit(solution)/shard_map/ppermute | solution.py:36
  147.6 0.3 collective-permute-start.8
  147.9 1.8 collective-permute-done.10
  149.7 3.5 %collective-permute-done.8 = f32[4,18,128]{2,1,0:T(8,128)S(1)} collective-permute-done((f32[4,18,128]{2,1,0:T(8,128)S(1)}, f32[4,18,128]{2,1,0:T(8,128)S(1)}, u32[]{:S(2)}, u32[]{:S(2)}) %collective-permute-start.8) | collective-permute-done | bytes 36896 | tf_op jit(solution)/shard_map/ppermute | solution.py:36
  153.2 2.1 %collective-permute-start.11 = (f32[4,16,128]{2,1,0:T(8,128)S(1)}, f32[4,16,128]{2,1,0:T(8,128)S(1)}, u32[]{:S(2)}, u32[]{:S(2)}) collective-permute-start(f32[4,16,128]{2,1,0:T(8,128)S(1)} %slice.78), channel_id=1, source_target_pairs={{0,32},{32,0},{64,96},{96,64},{128,160},{160,128},{192,224},{224,1... | collective-permute-start | bytes 98312 | tf_op jit(solution)/shard_map/ppermute | solution.py:59
  155.3 3.9 %collective-permute-done.11 = f32[4,16,128]{2,1,0:T(8,128)S(1)} collective-permute-done((f32[4,16,128]{2,1,0:T(8,128)S(1)}, f32[4,16,128]{2,1,0:T(8,128)S(1)}, u32[]{:S(2)}, u32[]{:S(2)}) %collective-permute-start.11) | collective-permute-done | bytes 32800 | tf_op jit(solution)/shard_map/ppermute | solution.py:59
  159.2 1.4 collective-permute-start.12
  160.7 3.3 %collective-permute-done.12 = f32[4,16,128]{2,1,0:T(8,128)S(1)} collective-permute-done((f32[4,16,128]{2,1,0:T(8,128)S(1)}, f32[4,16,128]{2,1,0:T(8,128)S(1)}, u32[]{:S(2)}, u32[]{:S(2)}) %collective-permute-start.12) | collective-permute-done | bytes 32800 | tf_op jit(solution)/shard_map/ppermute | solution.py:59
  164.0 4.8 %collective-permute-start.13 = (f32[4,16,128]{2,1,0:T(8,128)S(1)}, f32[4,16,128]{2,1,0:T(8,128)S(1)}, u32[]{:S(2)}, u32[]{:S(2)}) collective-permute-start(f32[4,16,128]{2,1,0:T(8,128)S(1)} %add.182.left_ref), channel_id=1, source_target_pairs={{0,128},{32,160},{64,192},{96,224},{128,0},{160,32},{192,64},{224,... | collective-permute-start | bytes 98312 | tf_op jit(solution)/shard_map/ppermute | solution.py:59
  168.8 0.6 slice_select_fusion
  169.5 2.4 %collective-permute-done.13.right_ref = f32[4,16,128]{2,1,0:T(8,128)S(1)} collective-permute-done((f32[4,16,128]{2,1,0:T(8,128)S(1)}, f32[4,16,128]{2,1,0:T(8,128)S(1)}, u32[]{:S(2)}, u32[]{:S(2)}) %collective-permute-start.13) | collective-permute-done | bytes 32800 | tf_op jit(solution)/shard_map/ppermute | solution.py:59
  171.8 1.1 collective-permute-start.16
  173.0 2.9 %collective-permute-start.15 = (f32[4,16,128]{2,1,0:T(8,128)S(1)}, f32[4,16,128]{2,1,0:T(8,128)S(1)}, u32[]{:S(2)}, u32[]{:S(2)}) collective-permute-start(f32[4,16,128]{2,1,0:T(8,128)S(1)} %shard_map.94), channel_id=1, source_target_pairs={{16,0},{18,2},{20,4},{22,6},{24,8},{26,10},{28,12},{30,14},{0,16},... | collective-permute-start | bytes 98312 | tf_op jit(solution)/shard_map/ppermute | solution.py:31
  175.9 0.6 collective-permute-start.14
  176.4 1.8 fusion.32
  178.2 1.6 collective-permute-done.14
  179.9 0.7 reshape.260
  (79 shorter events, 1.9 us)
Async XLA Ops:
  7.2 31.4 %copy-start = (bf16[256,2048]{1,0:T(8,128)(2,1)S(1)}, bf16[256,2048]{1,0:T(8,128)(2,1)}, u32[]{:S(2)}) copy-start(bf16[256,2048]{1,0:T(8,128)(2,1)} %param.7) | copy-start | bytes 3145732
  7.2 86.9 %all-gather.2.cloned.1.call-start = ((), (), s32[]{:S(2)}) async-start(), calls=%async_computation.4 | async-start | bytes 10027008 | tf_op jit(solution)/shard_map/all_gather | solution.py:81
  10.2 26.7 %all-to-all-start = ((s32[128,1,2]{2,1,0:T(1,128)}), s32[128,1,2]{2,1,0:T(1,128)S(1)}, u32[]{:S(2)}, u32[]{:S(2)}) async-start(s32[128,1,2]{2,1,0:T(1,128)} %copy.24), calls=%async_computation | async-start | bytes 131072 | tf_op jit(solution)/shard_map/all_to_all | solution.py:18
  40.0 31.6 %copy-start.3 = (bf16[2048,16]{0,1:T(8,128)(2,1)S(1)}, bf16[2048,16]{0,1:T(8,128)(2,1)}, u32[]{:S(2)}) copy-start(bf16[2048,16]{0,1:T(8,128)(2,1)} %param.8) | copy-start | bytes 196612
  40.1 33.1 %copy-start.2 = (bf16[16,2048]{1,0:T(8,128)(2,1)S(1)}, bf16[16,2048]{1,0:T(8,128)(2,1)}, u32[]{:S(2)}) copy-start(bf16[16,2048]{1,0:T(8,128)(2,1)} %param.9) | copy-start | bytes 196612
  71.6 22.5 %copy-start.4 = (f32[2048]{0:T(1024)S(1)}, f32[2048]{0:T(1024)}, u32[]{:S(2)}) copy-start(f32[2048]{0:T(1024)} %param.10) | copy-start | bytes 24580
  72.0 1.2 collective-permute-start
  75.8 1.1 collective-permute-start.1
  94.1 4.8 %copy-start.1 = (f32[256,2048]{1,0:T(8,128)S(1)}, f32[256,2048]{1,0:T(8,128)}, u32[]{:S(2)}) copy-start(f32[256,2048]{1,0:T(8,128)} %get-tuple-element.20) | copy-start | bytes 6291460
  98.8 5.2 %collective-permute-start.2 = (f32[1152,256]{0,1:T(8,128)S(1)}, f32[1152,256]{0,1:T(8,128)S(1)}, u32[]{:S(2)}, u32[]{:S(2)}) collective-permute-start(f32[1152,256]{0,1:T(8,128)S(1)} %fusion.4), channel_id=1, source_target_pairs={{0,1},{1,0},{2,3},{3,2},{4,5},{5,4},{6,7},{7,6},{8,9},{9,8},{10,11... | collective-permute-start | bytes 3538952 | tf_op jit(solution)/shard_map/ppermute | solution.py:22
  98.9 22.6 %slice-start = ((s8[9437184]{0:T(1024)(128)(4,1)}), s8[4194304]{0:T(1024)(128)(4,1)S(1)}, s32[]{:S(2)}) async-start(s8[9437184]{0:T(1024)(128)(4,1)} %bitcast.100), calls=%async_computation.5 | async-start | bytes 8388608
  98.9 22.6 %slice-start.1 = ((s8[9437184]{0:T(1024)(128)(4,1)}), s8[4194304]{0:T(1024)(128)(4,1)S(1)}, s32[]{:S(2)}) async-start(s8[9437184]{0:T(1024)(128)(4,1)} %bitcast.100), calls=%async_computation.6 | async-start | bytes 8388608
  103.1 3.2 %collective-permute-start.3 = (f32[1152,256]{0,1:T(8,128)S(1)}, f32[1152,256]{0,1:T(8,128)S(1)}, u32[]{:S(2)}, u32[]{:S(2)}) collective-permute-start(f32[1152,256]{0,1:T(8,128)S(1)} %fusion.7), channel_id=1, source_target_pairs={{0,1},{1,0},{2,3},{3,2},{4,5},{5,4},{6,7},{7,6},{8,9},{9,8},{10,11... | collective-permute-start | bytes 3538952 | tf_op jit(solution)/shard_map/ppermute | solution.py:22
  104.1 17.4 %slice-start.2 = ((s8[9437184]{0:T(1024)(128)(4,1)}), s8[1048576]{0:T(1024)(128)(4,1)S(1)}, s32[]{:S(2)}) async-start(s8[9437184]{0:T(1024)(128)(4,1)} %bitcast.100), calls=%async_computation.7 | async-start | bytes 2097152
  125.9 7.1 %collective-permute-start.4 = (f32[256,1]{0,1:T(1,128)S(1)}, f32[256,1]{0,1:T(1,128)S(1)}, u32[]{:S(2)}, u32[]{:S(2)}) collective-permute-start(f32[256,1]{0,1:T(1,128)S(1)} %bitcast.97), channel_id=1, source_target_pairs={{0,1},{1,0},{2,3},{3,2},{4,5},{5,4},{6,7},{7,6},{8,9},{9,8},{10,11... | collective-permute-start | bytes 3080 | tf_op jit(solution)/shard_map/ppermute | solution.py:22
  126.0 45.9 %all-to-all-start.3 = ((bf16[8,32,2048]{2,1,0:T(8,128)(2,1)}), bf16[8,32,2048]{2,1,0:T(8,128)(2,1)S(1)}, u32[]{:S(2)}, u32[]{:S(2)}) async-start(bf16[8,32,2048]{2,1,0:T(8,128)(2,1)} %bitcast.22), calls=%async_computation.3 | async-start | bytes 2097152 | tf_op jit(solution)/shard_map/all_to_all | solution.py:18
  136.7 4.5 %collective-permute-start.5 = (f32[4,18,128]{2,1,0:T(8,128)S(1)}, f32[4,18,128]{2,1,0:T(8,128)S(1)}, u32[]{:S(2)}, u32[]{:S(2)}) collective-permute-start(f32[4,18,128]{2,1,0:T(8,128)S(1)} %get-tuple-element.12), channel_id=1, source_target_pairs={{8,0},{10,2},{12,4},{14,6},{16,8},{18,10},{20,12},{22,14},{24,16},... | collective-permute-start | bytes 110600 | tf_op jit(solution)/shard_map/ppermute | solution.py:31
  138.7 5.6 %collective-permute-start.6 = (f32[4,18,128]{2,1,0:T(8,128)S(1)}, f32[4,18,128]{2,1,0:T(8,128)S(1)}, u32[]{:S(2)}, u32[]{:S(2)}) collective-permute-start(f32[4,18,128]{2,1,0:T(8,128)S(1)} %get-tuple-element.13), channel_id=1, source_target_pairs={{16,0},{18,2},{20,4},{22,6},{24,8},{26,10},{28,12},{30,14},{0,16},... | collective-permute-start | bytes 110600 | tf_op jit(solution)/shard_map/ppermute | solution.py:31
  139.3 4.9 %collective-permute-start.7 = (f32[4,18,128]{2,1,0:T(8,128)S(1)}, f32[4,18,128]{2,1,0:T(8,128)S(1)}, u32[]{:S(2)}, u32[]{:S(2)}) collective-permute-start(f32[4,18,128]{2,1,0:T(8,128)S(1)} %get-tuple-element.14), channel_id=1, source_target_pairs={{24,0},{26,2},{28,4},{30,6},{0,8},{2,10},{4,12},{6,14},{8,16},{10,... | collective-permute-start | bytes 110600 | tf_op jit(solution)/shard_map/ppermute | solution.py:31
  144.3 5.4 %collective-permute-start.10 = (f32[4,18,128]{2,1,0:T(8,128)S(1)}, f32[4,18,128]{2,1,0:T(8,128)S(1)}, u32[]{:S(2)}, u32[]{:S(2)}) collective-permute-start(f32[4,18,128]{2,1,0:T(8,128)S(1)} %fusion.41), channel_id=1, source_target_pairs={{6,0},{0,2},{2,4},{4,6},{14,8},{8,10},{10,12},{12,14},{22,16},{16,... | collective-permute-start | bytes 110600 | tf_op jit(solution)/shard_map/ppermute | solution.py:36
  144.7 4.9 %collective-permute-start.9 = (f32[4,18,128]{2,1,0:T(8,128)S(1)}, f32[4,18,128]{2,1,0:T(8,128)S(1)}, u32[]{:S(2)}, u32[]{:S(2)}) collective-permute-start(f32[4,18,128]{2,1,0:T(8,128)S(1)} %fusion.41), channel_id=1, source_target_pairs={{2,0},{4,2},{6,4},{0,6},{10,8},{12,10},{14,12},{8,14},{18,16},{20,... | collective-permute-start | bytes 110600 | tf_op jit(solution)/shard_map/ppermute | solution.py:36
  147.6 5.6 %collective-permute-start.8 = (f32[4,18,128]{2,1,0:T(8,128)S(1)}, f32[4,18,128]{2,1,0:T(8,128)S(1)}, u32[]{:S(2)}, u32[]{:S(2)}) collective-permute-start(f32[4,18,128]{2,1,0:T(8,128)S(1)} %fusion.41), channel_id=1, source_target_pairs={{4,0},{6,2},{0,4},{2,6},{12,8},{14,10},{8,12},{10,14},{20,16},{22,... | collective-permute-start | bytes 110600 | tf_op jit(solution)/shard_map/ppermute | solution.py:36
  153.2 6.0 %collective-permute-start.11 = (f32[4,16,128]{2,1,0:T(8,128)S(1)}, f32[4,16,128]{2,1,0:T(8,128)S(1)}, u32[]{:S(2)}, u32[]{:S(2)}) collective-permute-start(f32[4,16,128]{2,1,0:T(8,128)S(1)} %slice.78), channel_id=1, source_target_pairs={{0,32},{32,0},{64,96},{96,64},{128,160},{160,128},{192,224},{224,1... | collective-permute-start | bytes 98312 | tf_op jit(solution)/shard_map/ppermute | solution.py:59
  159.2 4.8 %collective-permute-start.12 = (f32[4,16,128]{2,1,0:T(8,128)S(1)}, f32[4,16,128]{2,1,0:T(8,128)S(1)}, u32[]{:S(2)}, u32[]{:S(2)}) collective-permute-start(f32[4,16,128]{2,1,0:T(8,128)S(1)} %slice_add_fusion), channel_id=1, source_target_pairs={{0,64},{32,96},{64,0},{96,32},{128,192},{160,224},{192,128},{224,1... | collective-permute-start | bytes 98312 | tf_op jit(solution)/shard_map/ppermute | solution.py:59
  164.0 7.8 %collective-permute-start.13 = (f32[4,16,128]{2,1,0:T(8,128)S(1)}, f32[4,16,128]{2,1,0:T(8,128)S(1)}, u32[]{:S(2)}, u32[]{:S(2)}) collective-permute-start(f32[4,16,128]{2,1,0:T(8,128)S(1)} %add.182.left_ref), channel_id=1, source_target_pairs={{0,128},{32,160},{64,192},{96,224},{128,0},{160,32},{192,64},{224,... | collective-permute-start | bytes 98312 | tf_op jit(solution)/shard_map/ppermute | solution.py:59
  171.8 7.9 %collective-permute-start.16 = (f32[4,16,128]{2,1,0:T(8,128)S(1)}, f32[4,16,128]{2,1,0:T(8,128)S(1)}, u32[]{:S(2)}, u32[]{:S(2)}) collective-permute-start(f32[4,16,128]{2,1,0:T(8,128)S(1)} %shard_map.94), channel_id=1, source_target_pairs={{24,0},{26,2},{28,4},{30,6},{0,8},{2,10},{4,12},{6,14},{8,16},{10,... | collective-permute-start | bytes 98312 | tf_op jit(solution)/shard_map/ppermute | solution.py:31
  173.0 6.8 %collective-permute-start.15 = (f32[4,16,128]{2,1,0:T(8,128)S(1)}, f32[4,16,128]{2,1,0:T(8,128)S(1)}, u32[]{:S(2)}, u32[]{:S(2)}) collective-permute-start(f32[4,16,128]{2,1,0:T(8,128)S(1)} %shard_map.94), channel_id=1, source_target_pairs={{16,0},{18,2},{20,4},{22,6},{24,8},{26,10},{28,12},{30,14},{0,16},... | collective-permute-start | bytes 98312 | tf_op jit(solution)/shard_map/ppermute | solution.py:31
  175.9 3.9 %collective-permute-start.14 = (f32[4,16,128]{2,1,0:T(8,128)S(1)}, f32[4,16,128]{2,1,0:T(8,128)S(1)}, u32[]{:S(2)}, u32[]{:S(2)}) collective-permute-start(f32[4,16,128]{2,1,0:T(8,128)S(1)} %shard_map.94), channel_id=1, source_target_pairs={{8,0},{10,2},{12,4},{14,6},{16,8},{18,10},{20,12},{22,14},{24,16},... | collective-permute-start | bytes 98312 | tf_op jit(solution)/shard_map/ppermute | solution.py:31
Sparse Core Ops, SparseCore 0:
  10.5 83.5 all-gather.1

commit v4 on v3

--- a/solution.py
+++ b/solution.py
@@ -110,11 +110,12 @@
     squares = squares + swap(squares)
     rinv = lax.rsqrt(squares / MODEL_WIDTH + EPS)
     hist = (pre * rinv * embedding_norm_gain).astype(jnp.bfloat16)
+    hist = lax.optimization_barrier(hist)
 
     line = jnp.arange(group, dtype=jnp.int32)
     valid = line % LEN != LEN - 1
     hit = (line[:, None] + 1 == position[None, :]) & valid[:, None]
-    cut = group // 2
+    cut = group // 3 * 2
     partials = [
         lax.dot_general(
             part, hist, (((1,), (1,)), ((), ())), preferred_element_type=jnp.float32
@@ -149,7 +150,7 @@
     inner = jnp.sum(pre * scaled, axis=1, keepdims=True)
     inner = (inner + swap(inner)) / MODEL_WIDTH
     dpre = rinv * scaled - pre * rinv * rinv * rinv * inner
-    b_part = jnp.dot(low.T, dpre, precision=lax.Precision.HIGHEST)
+    b_part = jnp.dot(low.T, dpre, precision=lax.Precision.HIGH)
     rank = b_part.shape[0]
     share = part_width // users
     b_part = b_part.reshape(rank, users, share).transpose(1, 0, 2)
@@ -163,8 +164,7 @@
     own = lax.dynamic_slice_in_dim(lse, me * count, count, 0)
     pos_loss = jnp.where(valid[:count], own - positive, 0.0)
     b_part = both[:, :rank]
-    for mask in (1, 2):
-        b_part = b_part + plane_pair(b_part, mask)
+    b_part = (b_part + plane_pair(b_part, 1)) + (plane_pair(b_part, 2) + plane_pair(b_part, 3))
     b_part = add_after(b_part, plane_pair(b_part, 4), [returned])
     b_grad = jnp.stack([b_part] + [from_x(b_part, step) for step in (1, 2, 3)])
     b_grad = turn(b_grad, (4 - my_x) % 4)

time: 188 us -> 183 us (0.973)
  matrix products: 21.4 us -> 16.8 us
  waiting for transfers between devices: 53 us -> 49.8 us
  other arithmetic: 5.42 us -> 7.59 us
    dot_general x2, matrix products: 8.8 us -> 6.09 us  [body(): lax.dot_general(part, hist, (((1,), (1,)), ((), ())), preferred_element_t...]
    ppermute x3 -> x4, waiting for transfers between devices: 9.54 us -> 7.34 us  [plane_pair(): return lax.ppermute(x, 'item', [(z, z ^ mask) for z in range(planes)])]
    ppermute x3 -> x4, starting transfers between devices: 8.33 us -> 8.88 us  [plane_pair(): return lax.ppermute(x, 'item', [(z, z ^ mask) for z in range(planes)])]
  transfers between devices with their start and end apart: 20 -> 21, of which waited for: 12 -> 12; matrix products, arithmetic and copies ran while one was open for 10% -> 9% of each run, Pallas kernels for 0% -> 0%
where the time goes in v4:
time: 183 us
  waiting for transfers between devices  49.8 us (27%)
  starting transfers between devices  44.8 us (24%)
  blocking collectives  44.4 us (24%)
  matrix products  16.8 us (9%)
  between operations  14.5 us (8%)
  other arithmetic  7.59 us (4%)
  local copies, waits for them, and re-layouts  5.08 us (3%)
    all_to_all x2, blocking collectives, exchange(): return lax.all_to_all(x, axis, split_axis=0, concat_axis=0, tiled=True)  44.4 us
    all_to_all x2, starting transfers between devices, exchange(): return lax.all_to_all(x, axis, split_axis=0, concat_axis=0, tiled=True)  22.5 us
    all_gather x1, waiting for transfers between devices, body(): queries = lax.all_gather(user_context_state, 'user', axis=0, tiled=True)  17.1 us
    all_to_all x2, waiting for transfers between devices, exchange(): return lax.all_to_all(x, axis, split_axis=0, concat_axis=0, tiled=True)  11.3 us
    ppermute x6, starting transfers between devices, from_x(): return lax.ppermute(x, 'user', pairs)  9.21 us
    ppermute x4, starting transfers between devices, plane_pair(): return lax.ppermute(x, 'item', [(z, z ^ mask) for z in range(planes)])  8.88 us
    ppermute x4, waiting for transfers between devices, plane_pair(): return lax.ppermute(x, 'item', [(z, z ^ mask) for z in range(planes)])  7.34 us
    dot_general x2, matrix products, body(): lax.dot_general(part, hist, (((1,), (1,)), ((), ())), preferred_element_t...  6.09 us
  transfers between devices with their start and end apart: 21, of which 12 were waited for; matrix products, arithmetic and copies ran while one was open for 9% of the time, Pallas kernels for 0%

profile of v4, /device:TPU:2, one launch (start us, length us, event | category | flops | bytes accessed | tf_op | source)
XLA Modules:
  0.0 183.0 jit_solution(12954454896288550140)
XLA Ops:
  7.2 0.7 all-gather.2.cloned.1.call-update
  7.9 0.7 multiply_add_fusion
  8.6 0.8 select_reduce_fusion.3
  9.4 0.7 copy.24
  10.2 15.4 %all-to-all-start = ((s32[128,1,2]{2,1,0:T(1,128)}), s32[128,1,2]{2,1,0:T(1,128)S(1)}, u32[]{:S(2)}, u32[]{:S(2)}) async-start(s32[128,1,2]{2,1,0:T(1,128)} %copy.24), calls=%async_computation | async-start | bytes 131072 | tf_op jit(solution)/shard_map/all_to_all | solution.py:18
  25.6 11.3 %all-to-all-done = s32[128,1,2]{2,1,0:T(1,128)S(1)} async-done(((s32[128,1,2]{2,1,0:T(1,128)}), s32[128,1,2]{2,1,0:T(1,128)S(1)}, u32[]{:S(2)}, u32[]{:S(2)}) %all-to-all-start) | async-done | bytes 1056 | tf_op jit(solution)/shard_map/all_to_all | solution.py:18
  37.0 0.5 broadcast.300
  37.5 0.8 reduce.8
  38.5 1.4 gather_fusion
  40.1 31.5 %all_to_all.24 = bf16[8,32,2176]{2,1,0:T(8,128)(2,1)S(1)} all-to-all(bf16[8,32,2176]{2,1,0:T(8,128)(2,1)S(1)} %bitcast.87), channel_id=1, replica_groups=mesh['item'=8,'user'=16,'mp'=2] {'item'}, dimensions={0} | all-to-all | bytes 2228224 | tf_op jit(solution)/shard_map/all_to_all | solution.py:18
  71.7 0.4 fusion.30
  72.0 1.2 collective-permute-done
  73.2 1.3 multiply_reduce_fusion.1
  74.8 1.0 collective-permute-done.1
  75.8 1.2 multiply_convert_fusion
  77.0 17.1 %all-gather.2.cloned.1.call-done = bf16[2304,2048]{1,0:T(8,128)(2,1)} async-done(((bf16[144,2048]{1,0:T(8,128)(2,1)}), bf16[2304,2048]{1,0:T(8,128)(2,1)}) %all-gather.2.cloned.1.call-update) | async-done | bytes 9437200 | tf_op jit(solution)/shard_map/all_gather | solution.py:81
  94.1 5.1 %fusion.4 = f32[1536,256]{0,1:T(8,128)S(1)} fusion(bf16[256,2048]{1,0:T(8,128)(2,1)} %multiply_convert_fusion, bf16[2304,2048]{1,0:T(8,128)(2,1)} %all-gather.2.cloned.1.call-done), kind=kOutput, calls=%fused_computation.5 | convolution fusion | flops 1610612736 | bytes 8912896 | tf_op jit(solution)/shard_map/dot_general | solution.py:120
  99.3 0.9 copy-done.6
  100.2 1.0 fusion.15
  101.6 1.0 convert_reduce_fusion
  102.6 1.3 collective-permute-done.3
  104.2 0.3 fusion.53
  104.5 1.2 select_reduce_fusion.1
  105.9 12.9 %all_to_all.25 = f32[16,2,2304]{2,1,0:T(2,128)S(1)} all-to-all(f32[16,2,2304]{2,1,0:T(2,128)S(1)} %broadcast_in_dim.127), channel_id=1, replica_groups=mesh['item'=8,'user'=16,'mp'=2] {'user'}, dimensions={0} | all-to-all | bytes 589824 | tf_op jit(solution)/shard_map/all_to_all | solution.py:18
  119.1 4.3 %multiply_reduce_fusion = (f32[256]{0:T(256)S(1)}, bf16[256,2048]{1,0:T(8,128)(2,1)}) fusion(f32[256,2048]{1,0:T(8,128)S(1)} %get-tuple-element.20, f32[2048]{0:T(1024)S(1)} %copy-done.5, bf16[2304,2048]{1,0:T(8,128)(2,1)S(1)} %copy-done.6, s32[2304]{0:T(1024)S(1)} %iota_add_fusion, f32[2304]{0:T(1024)S(1)} %get-tuple-element.8, ...), kind=kOutput, calls=%fused_computation.17 | convolution fusion | flops 2425028352 | bytes 14973440 | tf_op jit(solution)/shard_map/dot_general | solution.py:138
  123.5 7.0 %all-to-all-start.3 = ((bf16[8,32,2048]{2,1,0:T(8,128)(2,1)}), bf16[8,32,2048]{2,1,0:T(8,128)(2,1)S(1)}, u32[]{:S(2)}, u32[]{:S(2)}) async-start(bf16[8,32,2048]{2,1,0:T(8,128)(2,1)} %bitcast.89), calls=%async_computation.3 | async-start | bytes 2097152 | tf_op jit(solution)/shard_map/all_to_all | solution.py:18
  130.5 3.0 %fusion.24 = f32[2,16,8,128]{3,2,1,0:T(8,128)S(1)} fusion(f32[256,16]{0,1:T(8,128)S(1)} %add.161, bf16[256,2048]{1,0:T(8,128)(2,1)} %get-tuple-element.22, f32[256,2048]{1,0:T(8,128)} %copy-done.1, f32[256]{0:T(256)S(1)} %bitcast.101, f32[2048]{0:T(1024)S(1)} %copy-done.5, f32[256]{0:T(256)S(1)} %bitcast.94), kind=kOutput, calls=%fused_computation.32 | convolution fusion | flops 54525952 | bytes 3303424 | tf_op jit(solution)/shard_map/dot_general | solution.py:153
  133.7 1.9 %collective-permute-start.5 = (f32[4,18,128]{2,1,0:T(8,128)S(1)}, f32[4,18,128]{2,1,0:T(8,128)S(1)}, u32[]{:S(2)}, u32[]{:S(2)}) collective-permute-start(f32[4,18,128]{2,1,0:T(8,128)S(1)} %get-tuple-element.12), channel_id=1, source_target_pairs={{8,0},{10,2},{12,4},{14,6},{16,8},{18,10},{20,12},{22,14},{24,16},... | collective-permute-start | bytes 110600 | tf_op jit(solution)/shard_map/ppermute | solution.py:31
  135.6 0.8 collective-permute-start.6
  136.4 1.8 collective-permute-start.7
  138.2 3.1 %collective-permute-done.6 = f32[4,18,128]{2,1,0:T(8,128)S(1)} collective-permute-done((f32[4,18,128]{2,1,0:T(8,128)S(1)}, f32[4,18,128]{2,1,0:T(8,128)S(1)}, u32[]{:S(2)}, u32[]{:S(2)}) %collective-permute-start.6) | collective-permute-done | bytes 36896 | tf_op jit(solution)/shard_map/ppermute | solution.py:31
  141.2 0.5 collective-permute-start.10
  141.7 2.9 %collective-permute-start.9 = (f32[4,18,128]{2,1,0:T(8,128)S(1)}, f32[4,18,128]{2,1,0:T(8,128)S(1)}, u32[]{:S(2)}, u32[]{:S(2)}) collective-permute-start(f32[4,18,128]{2,1,0:T(8,128)S(1)} %fusion.41), channel_id=1, source_target_pairs={{2,0},{4,2},{6,4},{0,6},{10,8},{12,10},{14,12},{8,14},{18,16},{20,... | collective-permute-start | bytes 110600 | tf_op jit(solution)/shard_map/ppermute | solution.py:36
  144.8 1.8 collective-permute-done.10
  146.6 3.5 %collective-permute-done.8 = f32[4,18,128]{2,1,0:T(8,128)S(1)} collective-permute-done((f32[4,18,128]{2,1,0:T(8,128)S(1)}, f32[4,18,128]{2,1,0:T(8,128)S(1)}, u32[]{:S(2)}, u32[]{:S(2)}) %collective-permute-start.8) | collective-permute-done | bytes 36896 | tf_op jit(solution)/shard_map/ppermute | solution.py:36
  150.2 3.2 %collective-permute-start.12 = (f32[4,16,128]{2,1,0:T(8,128)S(1)}, f32[4,16,128]{2,1,0:T(8,128)S(1)}, u32[]{:S(2)}, u32[]{:S(2)}) collective-permute-start(f32[4,16,128]{2,1,0:T(8,128)S(1)} %slice.78), channel_id=1, source_target_pairs={{0,64},{32,96},{64,0},{96,32},{128,192},{160,224},{192,128},{224,1... | collective-permute-start | bytes 98312 | tf_op jit(solution)/shard_map/ppermute | solution.py:59
  153.4 1.5 collective-permute-start.13
  155.0 2.7 %collective-permute-done.12 = f32[4,16,128]{2,1,0:T(8,128)S(1)} collective-permute-done((f32[4,16,128]{2,1,0:T(8,128)S(1)}, f32[4,16,128]{2,1,0:T(8,128)S(1)}, u32[]{:S(2)}, u32[]{:S(2)}) %collective-permute-start.12) | collective-permute-done | bytes 32800 | tf_op jit(solution)/shard_map/ppermute | solution.py:59
  157.7 1.6 collective-permute-done.13
  159.2 4.2 %collective-permute-start.14 = (f32[4,16,128]{2,1,0:T(8,128)S(1)}, f32[4,16,128]{2,1,0:T(8,128)S(1)}, u32[]{:S(2)}, u32[]{:S(2)}) collective-permute-start(f32[4,16,128]{2,1,0:T(8,128)S(1)} %add_add_fusion.1.left_ref), channel_id=1, source_target_pairs={{0,128},{32,160},{64,192},{96,224},{128,0},{160,32},{192,64},{224,... | collective-permute-start | bytes 98312 | tf_op jit(solution)/shard_map/ppermute | solution.py:59
  163.4 0.6 slice_select_fusion
  164.1 3.1 %collective-permute-done.14.right_ref = f32[4,16,128]{2,1,0:T(8,128)S(1)} collective-permute-done((f32[4,16,128]{2,1,0:T(8,128)S(1)}, f32[4,16,128]{2,1,0:T(8,128)S(1)}, u32[]{:S(2)}, u32[]{:S(2)}) %collective-permute-start.14) | collective-permute-done | bytes 32800 | tf_op jit(solution)/shard_map/ppermute | solution.py:59
  167.2 1.2 collective-permute-start.17
  168.3 3.0 %collective-permute-start.16 = (f32[4,16,128]{2,1,0:T(8,128)S(1)}, f32[4,16,128]{2,1,0:T(8,128)S(1)}, u32[]{:S(2)}, u32[]{:S(2)}) collective-permute-start(f32[4,16,128]{2,1,0:T(8,128)S(1)} %shard_map.94), channel_id=1, source_target_pairs={{16,0},{18,2},{20,4},{22,6},{24,8},{26,10},{28,12},{30,14},{0,16},... | collective-permute-start | bytes 98312 | tf_op jit(solution)/shard_map/ppermute | solution.py:31
  171.3 0.6 collective-permute-start.15
  171.9 1.8 fusion.32
  173.7 1.5 collective-permute-done.15
  175.4 0.7 reshape.260
  (80 shorter events, 2.7 us)
Async XLA Ops:
  7.2 31.4 %copy-start = (bf16[256,2048]{1,0:T(8,128)(2,1)S(1)}, bf16[256,2048]{1,0:T(8,128)(2,1)}, u32[]{:S(2)}) copy-start(bf16[256,2048]{1,0:T(8,128)(2,1)} %param.7) | copy-start | bytes 3145732
  7.2 86.9 %all-gather.2.cloned.1.call-start = ((), (), s32[]{:S(2)}) async-start(), calls=%async_computation.4 | async-start | bytes 10027008 | tf_op jit(solution)/shard_map/all_gather | solution.py:81
  10.2 26.7 %all-to-all-start = ((s32[128,1,2]{2,1,0:T(1,128)}), s32[128,1,2]{2,1,0:T(1,128)S(1)}, u32[]{:S(2)}, u32[]{:S(2)}) async-start(s32[128,1,2]{2,1,0:T(1,128)} %copy.24), calls=%async_computation | async-start | bytes 131072 | tf_op jit(solution)/shard_map/all_to_all | solution.py:18
  40.0 31.6 %copy-start.7 = (bf16[2048,16]{0,1:T(8,128)(2,1)S(1)}, bf16[2048,16]{0,1:T(8,128)(2,1)}, u32[]{:S(2)}) copy-start(bf16[2048,16]{0,1:T(8,128)(2,1)} %param.8) | copy-start | bytes 196612
  40.1 33.1 %copy-start.4 = (bf16[16,2048]{1,0:T(8,128)(2,1)S(1)}, bf16[16,2048]{1,0:T(8,128)(2,1)}, u32[]{:S(2)}) copy-start(bf16[16,2048]{1,0:T(8,128)(2,1)} %param.9) | copy-start | bytes 196612
  71.6 2.9 %copy-start.2 = (bf16[8,32,2176]{2,1,0:T(8,128)(2,1)}, bf16[8,32,2176]{2,1,0:T(8,128)(2,1)S(1)}, u32[]{:S(2)}) copy-start(bf16[8,32,2176]{2,1,0:T(8,128)(2,1)S(1)} %all_to_all.24) | copy-start | bytes 3342340
  71.7 4.1 %copy-start.5 = (f32[2048]{0:T(1024)S(1)}, f32[2048]{0:T(1024)}, u32[]{:S(2)}) copy-start(f32[2048]{0:T(1024)} %param.10) | copy-start | bytes 24580
  72.0 1.2 collective-permute-start
  74.5 44.6 %copy-start.1 = (f32[256,2048]{1,0:T(8,128)}, f32[256,2048]{1,0:T(8,128)S(1)}, u32[]{:S(2)}) copy-start(f32[256,2048]{1,0:T(8,128)S(1)} %get-tuple-element.20) | copy-start | bytes 6291460
  74.5 1.2 collective-permute-start.1
  94.1 5.2 %copy-start.3 = (bf16[256,2048]{1,0:T(8,128)(2,1)S(1)}, bf16[256,2048]{1,0:T(8,128)(2,1)}, u32[]{:S(2)}) copy-start(bf16[256,2048]{1,0:T(8,128)(2,1)} %multiply_convert_fusion) | copy-start | bytes 3145732
  94.1 6.1 %copy-start.6 = (bf16[2304,2048]{1,0:T(8,128)(2,1)S(1)}, bf16[2304,2048]{1,0:T(8,128)(2,1)}, u32[]{:S(2)}) copy-start(bf16[2304,2048]{1,0:T(8,128)(2,1)} %all-gather.2.cloned.1.call-done) | copy-start | bytes 28311556
  99.2 4.7 %collective-permute-start.2 = (f32[1536,256]{0,1:T(8,128)S(1)}, f32[1536,256]{0,1:T(8,128)S(1)}, u32[]{:S(2)}, u32[]{:S(2)}) collective-permute-start(f32[1536,256]{0,1:T(8,128)S(1)} %fusion.4), channel_id=1, source_target_pairs={{0,1},{1,0},{2,3},{3,2},{4,5},{5,4},{6,7},{7,6},{8,9},{9,8},{10,11... | collective-permute-start | bytes 4718600 | tf_op jit(solution)/shard_map/ppermute | solution.py:22
  101.3 2.6 %collective-permute-start.3 = (f32[768,256]{0,1:T(8,128)S(1)}, f32[768,256]{0,1:T(8,128)S(1)}, u32[]{:S(2)}, u32[]{:S(2)}) collective-permute-start(f32[768,256]{0,1:T(8,128)S(1)} %fusion.15), channel_id=1, source_target_pairs={{0,1},{1,0},{2,3},{3,2},{4,5},{5,4},{6,7},{7,6},{8,9},{9,8},{10,11... | collective-permute-start | bytes 2359304 | tf_op jit(solution)/shard_map/ppermute | solution.py:22
  123.4 7.1 %collective-permute-start.4 = (f32[256,1]{0,1:T(1,128)S(1)}, f32[256,1]{0,1:T(1,128)S(1)}, u32[]{:S(2)}, u32[]{:S(2)}) collective-permute-start(f32[256,1]{0,1:T(1,128)S(1)} %bitcast.99), channel_id=1, source_target_pairs={{0,1},{1,0},{2,3},{3,2},{4,5},{5,4},{6,7},{7,6},{8,9},{9,8},{10,11... | collective-permute-start | bytes 3080 | tf_op jit(solution)/shard_map/ppermute | solution.py:22
  123.5 43.7 %all-to-all-start.3 = ((bf16[8,32,2048]{2,1,0:T(8,128)(2,1)}), bf16[8,32,2048]{2,1,0:T(8,128)(2,1)S(1)}, u32[]{:S(2)}, u32[]{:S(2)}) async-start(bf16[8,32,2048]{2,1,0:T(8,128)(2,1)} %bitcast.89), calls=%async_computation.3 | async-start | bytes 2097152 | tf_op jit(solution)/shard_map/all_to_all | solution.py:18
  133.7 4.5 %collective-permute-start.5 = (f32[4,18,128]{2,1,0:T(8,128)S(1)}, f32[4,18,128]{2,1,0:T(8,128)S(1)}, u32[]{:S(2)}, u32[]{:S(2)}) collective-permute-start(f32[4,18,128]{2,1,0:T(8,128)S(1)} %get-tuple-element.12), channel_id=1, source_target_pairs={{8,0},{10,2},{12,4},{14,6},{16,8},{18,10},{20,12},{22,14},{24,16},... | collective-permute-start | bytes 110600 | tf_op jit(solution)/shard_map/ppermute | solution.py:31
  135.6 5.6 %collective-permute-start.6 = (f32[4,18,128]{2,1,0:T(8,128)S(1)}, f32[4,18,128]{2,1,0:T(8,128)S(1)}, u32[]{:S(2)}, u32[]{:S(2)}) collective-permute-start(f32[4,18,128]{2,1,0:T(8,128)S(1)} %get-tuple-element.13), channel_id=1, source_target_pairs={{16,0},{18,2},{20,4},{22,6},{24,8},{26,10},{28,12},{30,14},{0,16},... | collective-permute-start | bytes 110600 | tf_op jit(solution)/shard_map/ppermute | solution.py:31
  136.4 4.8 %collective-permute-start.7 = (f32[4,18,128]{2,1,0:T(8,128)S(1)}, f32[4,18,128]{2,1,0:T(8,128)S(1)}, u32[]{:S(2)}, u32[]{:S(2)}) collective-permute-start(f32[4,18,128]{2,1,0:T(8,128)S(1)} %get-tuple-element.14), channel_id=1, source_target_pairs={{24,0},{26,2},{28,4},{30,6},{0,8},{2,10},{4,12},{6,14},{8,16},{10,... | collective-permute-start | bytes 110600 | tf_op jit(solution)/shard_map/ppermute | solution.py:31
  141.2 5.4 %collective-permute-start.10 = (f32[4,18,128]{2,1,0:T(8,128)S(1)}, f32[4,18,128]{2,1,0:T(8,128)S(1)}, u32[]{:S(2)}, u32[]{:S(2)}) collective-permute-start(f32[4,18,128]{2,1,0:T(8,128)S(1)} %fusion.41), channel_id=1, source_target_pairs={{6,0},{0,2},{2,4},{4,6},{14,8},{8,10},{10,12},{12,14},{22,16},{16,... | collective-permute-start | bytes 110600 | tf_op jit(solution)/shard_map/ppermute | solution.py:36
  141.7 4.9 %collective-permute-start.9 = (f32[4,18,128]{2,1,0:T(8,128)S(1)}, f32[4,18,128]{2,1,0:T(8,128)S(1)}, u32[]{:S(2)}, u32[]{:S(2)}) collective-permute-start(f32[4,18,128]{2,1,0:T(8,128)S(1)} %fusion.41), channel_id=1, source_target_pairs={{2,0},{4,2},{6,4},{0,6},{10,8},{12,10},{14,12},{8,14},{18,16},{20,... | collective-permute-start | bytes 110600 | tf_op jit(solution)/shard_map/ppermute | solution.py:36
  144.6 5.6 %collective-permute-start.8 = (f32[4,18,128]{2,1,0:T(8,128)S(1)}, f32[4,18,128]{2,1,0:T(8,128)S(1)}, u32[]{:S(2)}, u32[]{:S(2)}) collective-permute-start(f32[4,18,128]{2,1,0:T(8,128)S(1)} %fusion.41), channel_id=1, source_target_pairs={{4,0},{6,2},{0,4},{2,6},{12,8},{14,10},{8,12},{10,14},{20,16},{22,... | collective-permute-start | bytes 110600 | tf_op jit(solution)/shard_map/ppermute | solution.py:36
  150.2 7.5 %collective-permute-start.12 = (f32[4,16,128]{2,1,0:T(8,128)S(1)}, f32[4,16,128]{2,1,0:T(8,128)S(1)}, u32[]{:S(2)}, u32[]{:S(2)}) collective-permute-start(f32[4,16,128]{2,1,0:T(8,128)S(1)} %slice.78), channel_id=1, source_target_pairs={{0,64},{32,96},{64,0},{96,32},{128,192},{160,224},{192,128},{224,1... | collective-permute-start | bytes 98312 | tf_op jit(solution)/shard_map/ppermute | solution.py:59
  153.4 5.8 %collective-permute-start.13 = (f32[4,16,128]{2,1,0:T(8,128)S(1)}, f32[4,16,128]{2,1,0:T(8,128)S(1)}, u32[]{:S(2)}, u32[]{:S(2)}) collective-permute-start(f32[4,16,128]{2,1,0:T(8,128)S(1)} %slice.78), channel_id=1, source_target_pairs={{0,96},{32,64},{64,32},{96,0},{128,224},{160,192},{192,160},{224,1... | collective-permute-start | bytes 98312 | tf_op jit(solution)/shard_map/ppermute | solution.py:59
  154.9 4.4 %collective-permute-start.11 = (f32[4,16,128]{2,1,0:T(8,128)S(1)}, f32[4,16,128]{2,1,0:T(8,128)S(1)}, u32[]{:S(2)}, u32[]{:S(2)}) collective-permute-start(f32[4,16,128]{2,1,0:T(8,128)S(1)} %slice.78), channel_id=1, source_target_pairs={{0,32},{32,0},{64,96},{96,64},{128,160},{160,128},{192,224},{224,1... | collective-permute-start | bytes 98312 | tf_op jit(solution)/shard_map/ppermute | solution.py:59
  159.2 7.9 %collective-permute-start.14 = (f32[4,16,128]{2,1,0:T(8,128)S(1)}, f32[4,16,128]{2,1,0:T(8,128)S(1)}, u32[]{:S(2)}, u32[]{:S(2)}) collective-permute-start(f32[4,16,128]{2,1,0:T(8,128)S(1)} %add_add_fusion.1.left_ref), channel_id=1, source_target_pairs={{0,128},{32,160},{64,192},{96,224},{128,0},{160,32},{192,64},{224,... | collective-permute-start | bytes 98312 | tf_op jit(solution)/shard_map/ppermute | solution.py:59
  167.2 8.1 %collective-permute-start.17 = (f32[4,16,128]{2,1,0:T(8,128)S(1)}, f32[4,16,128]{2,1,0:T(8,128)S(1)}, u32[]{:S(2)}, u32[]{:S(2)}) collective-permute-start(f32[4,16,128]{2,1,0:T(8,128)S(1)} %shard_map.94), channel_id=1, source_target_pairs={{24,0},{26,2},{28,4},{30,6},{0,8},{2,10},{4,12},{6,14},{8,16},{10,... | collective-permute-start | bytes 98312 | tf_op jit(solution)/shard_map/ppermute | solution.py:31
  168.3 6.9 %collective-permute-start.16 = (f32[4,16,128]{2,1,0:T(8,128)S(1)}, f32[4,16,128]{2,1,0:T(8,128)S(1)}, u32[]{:S(2)}, u32[]{:S(2)}) collective-permute-start(f32[4,16,128]{2,1,0:T(8,128)S(1)} %shard_map.94), channel_id=1, source_target_pairs={{16,0},{18,2},{20,4},{22,6},{24,8},{26,10},{28,12},{30,14},{0,16},... | collective-permute-start | bytes 98312 | tf_op jit(solution)/shard_map/ppermute | solution.py:31
  171.3 3.9 %collective-permute-start.15 = (f32[4,16,128]{2,1,0:T(8,128)S(1)}, f32[4,16,128]{2,1,0:T(8,128)S(1)}, u32[]{:S(2)}, u32[]{:S(2)}) collective-permute-start(f32[4,16,128]{2,1,0:T(8,128)S(1)} %shard_map.94), channel_id=1, source_target_pairs={{8,0},{10,2},{12,4},{14,6},{16,8},{18,10},{20,12},{22,14},{24,16},... | collective-permute-start | bytes 98312 | tf_op jit(solution)/shard_map/ppermute | solution.py:31
Sparse Core Ops, SparseCore 0:
  10.5 83.5 all-gather.1

commit v5 on v4

--- a/solution.py
+++ b/solution.py
@@ -20,6 +20,16 @@
 
 def swap(x):
     return lax.ppermute(x, "mp", [(0, 1), (1, 0)])
+
+
+def thirds_product(x, y):
+    high = lax.reduce_precision(x, 8, 7)
+    middle = lax.reduce_precision(x - high, 8, 7)
+    parts = jnp.concatenate([high, middle, x - high - middle], axis=1).astype(jnp.bfloat16)
+    product = lax.dot_general(
+        parts, y, (((0,), (0,)), ((), ())), preferred_element_type=jnp.float32
+    )
+    return jnp.sum(product.reshape(3, x.shape[1], y.shape[1]), axis=0)
 
 
 def turn(x, by):
@@ -149,8 +159,14 @@
     scaled = hist_grad.astype(jnp.float32) * embedding_norm_gain
     inner = jnp.sum(pre * scaled, axis=1, keepdims=True)
     inner = (inner + swap(inner)) / MODEL_WIDTH
-    dpre = rinv * scaled - pre * rinv * rinv * rinv * inner
-    b_part = jnp.dot(low.T, dpre, precision=lax.Precision.HIGH)
+    bend = low * (rinv * rinv * rinv * inner)
+    b_part = thirds_product(low * rinv, hist_grad) * embedding_norm_gain
+    b_part = b_part - thirds_product(bend, hidden)
+    b_part = b_part - jnp.dot(
+        jnp.dot(bend.T, low, precision=lax.Precision.HIGHEST),
+        trained_up_weight.astype(jnp.float32),
+        precision=lax.Precision.HIGHEST,
+    )
     rank = b_part.shape[0]
     share = part_width // users
     b_part = b_part.reshape(rank, users, share).transpose(1, 0, 2)

time: 183 us -> 183 us (level)
  transfers between devices with their start and end apart: 21 -> 21, of which waited for: 12 -> 14; matrix products, arithmetic and copies ran while one was open for 9% -> 8% of each run, Pallas kernels for 0% -> 0%
where the time goes in v5:
time: 183 us; the launch traced here: 182 us
  waiting for transfers between devices  50.2 us (27%)
  starting transfers between devices  44.5 us (24%)
  blocking collectives  44.4 us (24%)
  matrix products  16.5 us (9%)
  between operations  14.5 us (8%)
  other arithmetic  6.83 us (4%)
  local copies, waits for them, and re-layouts  4.73 us (3%)
    all_to_all x2, blocking collectives, exchange(): return lax.all_to_all(x, axis, split_axis=0, concat_axis=0, tiled=True)  44.4 us
    all_to_all x2, starting transfers between devices, exchange(): return lax.all_to_all(x, axis, split_axis=0, concat_axis=0, tiled=True)  22.5 us
    all_gather x1, waiting for transfers between devices, body(): queries = lax.all_gather(user_context_state, 'user', axis=0, tiled=True)  18 us
    all_to_all x2, waiting for transfers between devices, exchange(): return lax.all_to_all(x, axis, split_axis=0, concat_axis=0, tiled=True)  11.3 us
    ppermute x6, starting transfers between devices, from_x(): return lax.ppermute(x, 'user', pairs)  9.26 us
    ppermute x4, starting transfers between devices, plane_pair(): return lax.ppermute(x, 'item', [(z, z ^ mask) for z in range(planes)])  8.59 us
    ppermute x4, waiting for transfers between devices, plane_pair(): return lax.ppermute(x, 'item', [(z, z ^ mask) for z in range(planes)])  7.39 us
    dot_general x2, matrix products, body(): lax.dot_general(part, hist, (((1,), (1,)), ((), ())), preferred_element_t...  5.9 us
  transfers between devices with their start and end apart: 21, of which 14 were waited for; matrix products, arithmetic and copies ran while one was open for 8% of the time, Pallas kernels for 0%

profile of v5, /device:TPU:2, one launch (start us, length us, event | category | flops | bytes accessed | tf_op | source)
XLA Modules:
  0.0 181.7 jit_solution(14016141052216696336)
XLA Ops:
  7.2 0.7 all-gather.2.cloned.1.call-update
  7.9 0.7 multiply_add_fusion
  8.6 0.8 select_reduce_fusion.3
  9.4 0.7 copy.24
  10.2 15.4 %all-to-all-start = ((s32[128,1,2]{2,1,0:T(1,128)}), s32[128,1,2]{2,1,0:T(1,128)S(1)}, u32[]{:S(2)}, u32[]{:S(2)}) async-start(s32[128,1,2]{2,1,0:T(1,128)} %copy.24), calls=%async_computation | async-start | bytes 131072 | tf_op jit(solution)/shard_map/all_to_all | solution.py:18
  25.6 11.3 %all-to-all-done = s32[128,1,2]{2,1,0:T(1,128)S(1)} async-done(((s32[128,1,2]{2,1,0:T(1,128)}), s32[128,1,2]{2,1,0:T(1,128)S(1)}, u32[]{:S(2)}, u32[]{:S(2)}) %all-to-all-start) | async-done | bytes 1056 | tf_op jit(solution)/shard_map/all_to_all | solution.py:18
  37.0 0.5 broadcast.300
  37.5 0.8 reduce.8
  38.5 1.4 gather_fusion
  40.1 31.5 %all_to_all.24 = bf16[8,32,2176]{2,1,0:T(8,128)(2,1)S(1)} all-to-all(bf16[8,32,2176]{2,1,0:T(8,128)(2,1)S(1)} %bitcast.93), channel_id=1, replica_groups=mesh['item'=8,'user'=16,'mp'=2] {'item'}, dimensions={0} | all-to-all | bytes 2228224 | tf_op jit(solution)/shard_map/all_to_all | solution.py:18
  72.0 1.2 collective-permute-done
  73.2 1.3 multiply_reduce_fusion.1
  74.8 1.0 collective-permute-done.1
  76.1 18.0 %all-gather.2.cloned.1.call-done = bf16[2304,2048]{1,0:T(8,128)(2,1)} async-done(((bf16[144,2048]{1,0:T(8,128)(2,1)}), bf16[2304,2048]{1,0:T(8,128)(2,1)}) %all-gather.2.cloned.1.call-update) | async-done | bytes 9437200 | tf_op jit(solution)/shard_map/all_gather | solution.py:91
  94.1 4.9 %fusion.4 = f32[1536,256]{0,1:T(8,128)S(1)} fusion(bf16[256,2048]{1,0:T(8,128)(2,1)S(1)} %multiply_convert_fusion, bf16[2304,2048]{1,0:T(8,128)(2,1)} %all-gather.2.cloned.1.call-done), kind=kOutput, calls=%fused_computation.5 | convolution fusion | flops 1610612736 | bytes 8912896 | tf_op jit(solution)/shard_map/dot_general | solution.py:130
  99.1 0.5 copy-done.5
  99.6 1.0 fusion.8
  101.1 2.5 %collective-permute-done.3 = f32[768,256]{0,1:T(8,128)S(1)} collective-permute-done((f32[768,256]{0,1:T(8,128)S(1)}, f32[768,256]{0,1:T(8,128)S(1)}, u32[]{:S(2)}, u32[]{:S(2)}) %collective-permute-start.3) | collective-permute-done | bytes 786464 | tf_op jit(solution)/shard_map/ppermute | solution.py:22
  104.3 1.2 select_reduce_fusion.1
  105.7 12.9 %all_to_all.25 = f32[16,2,2304]{2,1,0:T(2,128)S(1)} all-to-all(f32[16,2,2304]{2,1,0:T(2,128)S(1)} %broadcast_in_dim.128), channel_id=1, replica_groups=mesh['item'=8,'user'=16,'mp'=2] {'user'}, dimensions={0} | all-to-all | bytes 589824 | tf_op jit(solution)/shard_map/all_to_all | solution.py:18
  118.9 4.3 %multiply_reduce_fusion = (f32[256]{0:T(256)S(1)}, bf16[256,2048]{1,0:T(8,128)(2,1)}) fusion(f32[256,2048]{1,0:T(8,128)S(1)} %copy-done.2, f32[2048]{0:T(1024)S(1)} %copy-done.4, bf16[2304,2048]{1,0:T(8,128)(2,1)S(1)} %copy-done.5, s32[2304]{0:T(1024)S(1)} %iota_add_fusion, f32[2304]{0:T(1024)S(1)} %get-tuple-element.8, s32[256]{0:T(256)S(1)} %add_select_fusion.1, ...), kind=kOutput, calls=%fused_computation.15 | convolution fusion | flops 2425028352 | bytes 14973440 | tf_op jit(solution)/shard_map/dot_general | solution.py:148
  123.3 7.0 %all-to-all-start.3 = ((bf16[8,32,2048]{2,1,0:T(8,128)(2,1)}), bf16[8,32,2048]{2,1,0:T(8,128)(2,1)S(1)}, u32[]{:S(2)}, u32[]{:S(2)}) async-start(bf16[8,32,2048]{2,1,0:T(8,128)(2,1)} %bitcast.94), calls=%async_computation.3 | async-start | bytes 2097152 | tf_op jit(solution)/shard_map/all_to_all | solution.py:18
  130.3 1.0 fusion.18
  131.4 1.0 reduce_sum.68
  132.4 1.5 fusion.32
  134.5 1.2 collective-permute-start.7
  135.7 2.8 %collective-permute-start.6 = (f32[4,18,128]{2,1,0:T(8,128)S(1)}, f32[4,18,128]{2,1,0:T(8,128)S(1)}, u32[]{:S(2)}, u32[]{:S(2)}) collective-permute-start(f32[4,18,128]{2,1,0:T(8,128)S(1)} %get-tuple-element.13), channel_id=1, source_target_pairs={{16,0},{18,2},{20,4},{22,6},{24,8},{26,10},{28,12},{30,14},{0,16},... | collective-permute-start | bytes 110600 | tf_op jit(solution)/shard_map/ppermute | solution.py:41
  138.5 0.4 collective-permute-start.5
  138.9 2.5 %collective-permute-done.6 = f32[4,18,128]{2,1,0:T(8,128)S(1)} collective-permute-done((f32[4,18,128]{2,1,0:T(8,128)S(1)}, f32[4,18,128]{2,1,0:T(8,128)S(1)}, u32[]{:S(2)}, u32[]{:S(2)}) %collective-permute-start.6) | collective-permute-done | bytes 36896 | tf_op jit(solution)/shard_map/ppermute | solution.py:41
  141.4 1.1 collective-permute-done.5
  142.6 1.0 collective-permute-start.9
  143.6 1.1 collective-permute-start.10
  144.7 1.5 collective-permute-start.8
  146.1 0.6 collective-permute-done.9
  146.7 2.2 %collective-permute-done.10 = f32[4,18,128]{2,1,0:T(8,128)S(1)} collective-permute-done((f32[4,18,128]{2,1,0:T(8,128)S(1)}, f32[4,18,128]{2,1,0:T(8,128)S(1)}, u32[]{:S(2)}, u32[]{:S(2)}) %collective-permute-start.10) | collective-permute-done | bytes 36896 | tf_op jit(solution)/shard_map/ppermute | solution.py:46
  149.0 1.3 collective-permute-done.8
  150.3 3.0 %collective-permute-start.12 = (f32[4,16,128]{2,1,0:T(8,128)S(1)}, f32[4,16,128]{2,1,0:T(8,128)S(1)}, u32[]{:S(2)}, u32[]{:S(2)}) collective-permute-start(f32[4,16,128]{2,1,0:T(8,128)S(1)} %slice.78), channel_id=1, source_target_pairs={{0,64},{32,96},{64,0},{96,32},{128,192},{160,224},{192,128},{224,1... | collective-permute-start | bytes 98312 | tf_op jit(solution)/shard_map/ppermute | solution.py:69
  153.3 1.5 collective-permute-start.13
  154.9 2.9 %collective-permute-done.12 = f32[4,16,128]{2,1,0:T(8,128)S(1)} collective-permute-done((f32[4,16,128]{2,1,0:T(8,128)S(1)}, f32[4,16,128]{2,1,0:T(8,128)S(1)}, u32[]{:S(2)}, u32[]{:S(2)}) %collective-permute-start.12) | collective-permute-done | bytes 32800 | tf_op jit(solution)/shard_map/ppermute | solution.py:69
  157.8 1.3 collective-permute-done.13
  159.1 4.1 %collective-permute-start.14 = (f32[4,16,128]{2,1,0:T(8,128)S(1)}, f32[4,16,128]{2,1,0:T(8,128)S(1)}, u32[]{:S(2)}, u32[]{:S(2)}) collective-permute-start(f32[4,16,128]{2,1,0:T(8,128)S(1)} %add_add_fusion.1.left_ref), channel_id=1, source_target_pairs={{0,128},{32,160},{64,192},{96,224},{128,0},{160,32},{192,64},{224,... | collective-permute-start | bytes 98312 | tf_op jit(solution)/shard_map/ppermute | solution.py:69
  163.2 0.6 slice_select_fusion
  163.9 3.1 %collective-permute-done.14.right_ref = f32[4,16,128]{2,1,0:T(8,128)S(1)} collective-permute-done((f32[4,16,128]{2,1,0:T(8,128)S(1)}, f32[4,16,128]{2,1,0:T(8,128)S(1)}, u32[]{:S(2)}, u32[]{:S(2)}) %collective-permute-start.14) | collective-permute-done | bytes 32800 | tf_op jit(solution)/shard_map/ppermute | solution.py:69
  167.0 1.5 collective-permute-start.15
  168.6 0.8 collective-permute-start.16
  169.3 2.5 %collective-permute-start.17 = (f32[4,16,128]{2,1,0:T(8,128)S(1)}, f32[4,16,128]{2,1,0:T(8,128)S(1)}, u32[]{:S(2)}, u32[]{:S(2)}) collective-permute-start(f32[4,16,128]{2,1,0:T(8,128)S(1)} %shard_map.94), channel_id=1, source_target_pairs={{24,0},{26,2},{28,4},{30,6},{0,8},{2,10},{4,12},{6,14},{8,16},{10,... | collective-permute-start | bytes 98312 | tf_op jit(solution)/shard_map/ppermute | solution.py:41
  171.9 1.8 fusion.22
  174.1 0.7 reshape.268
  (84 shorter events, 4.3 us)
Async XLA Ops:
  7.2 31.4 %copy-start = (bf16[256,2048]{1,0:T(8,128)(2,1)S(1)}, bf16[256,2048]{1,0:T(8,128)(2,1)}, u32[]{:S(2)}) copy-start(bf16[256,2048]{1,0:T(8,128)(2,1)} %param.7) | copy-start | bytes 3145732
  7.2 86.9 %all-gather.2.cloned.1.call-start = ((), (), s32[]{:S(2)}) async-start(), calls=%async_computation.4 | async-start | bytes 10027008 | tf_op jit(solution)/shard_map/all_gather | solution.py:91
  10.2 26.7 %all-to-all-start = ((s32[128,1,2]{2,1,0:T(1,128)}), s32[128,1,2]{2,1,0:T(1,128)S(1)}, u32[]{:S(2)}, u32[]{:S(2)}) async-start(s32[128,1,2]{2,1,0:T(1,128)} %copy.24), calls=%async_computation | async-start | bytes 131072 | tf_op jit(solution)/shard_map/all_to_all | solution.py:18
  39.9 31.8 %copy-start.6 = (bf16[2048,16]{0,1:T(8,128)(2,1)S(1)}, bf16[2048,16]{0,1:T(8,128)(2,1)}, u32[]{:S(2)}) copy-start(bf16[2048,16]{0,1:T(8,128)(2,1)} %param.8) | copy-start | bytes 196612
  40.1 33.1 %copy-start.3 = (bf16[16,2048]{1,0:T(8,128)(2,1)S(1)}, bf16[16,2048]{1,0:T(8,128)(2,1)}, u32[]{:S(2)}) copy-start(bf16[16,2048]{1,0:T(8,128)(2,1)} %param.9) | copy-start | bytes 196612
  71.6 4.2 %copy-start.4 = (f32[2048]{0:T(1024)S(1)}, f32[2048]{0:T(1024)}, u32[]{:S(2)}) copy-start(f32[2048]{0:T(1024)} %param.10) | copy-start | bytes 24580
  72.0 1.2 collective-permute-start
  74.5 1.3 copy-start.1
  74.5 1.2 collective-permute-start.1
  94.1 5.5 %copy-start.5 = (bf16[2304,2048]{1,0:T(8,128)(2,1)S(1)}, bf16[2304,2048]{1,0:T(8,128)(2,1)}, u32[]{:S(2)}) copy-start(bf16[2304,2048]{1,0:T(8,128)(2,1)} %all-gather.2.cloned.1.call-done) | copy-start | bytes 28311556
  99.0 4.7 %collective-permute-start.2 = (f32[1536,256]{0,1:T(8,128)S(1)}, f32[1536,256]{0,1:T(8,128)S(1)}, u32[]{:S(2)}, u32[]{:S(2)}) collective-permute-start(f32[1536,256]{0,1:T(8,128)S(1)} %fusion.4), channel_id=1, source_target_pairs={{0,1},{1,0},{2,3},{3,2},{4,5},{5,4},{6,7},{7,6},{8,9},{9,8},{10,11... | collective-permute-start | bytes 4718600 | tf_op jit(solution)/shard_map/ppermute | solution.py:22
  100.7 3.0 %collective-permute-start.3 = (f32[768,256]{0,1:T(8,128)S(1)}, f32[768,256]{0,1:T(8,128)S(1)}, u32[]{:S(2)}, u32[]{:S(2)}) collective-permute-start(f32[768,256]{0,1:T(8,128)S(1)} %fusion.8), channel_id=1, source_target_pairs={{0,1},{1,0},{2,3},{3,2},{4,5},{5,4},{6,7},{7,6},{8,9},{9,8},{10,11... | collective-permute-start | bytes 2359304 | tf_op jit(solution)/shard_map/ppermute | solution.py:22
  104.3 14.6 %copy-start.2 = (f32[256,2048]{1,0:T(8,128)S(1)}, f32[256,2048]{1,0:T(8,128)}, u32[]{:S(2)}) copy-start(f32[256,2048]{1,0:T(8,128)} %copy-done.1) | copy-start | bytes 6291460
  123.2 7.1 %collective-permute-start.4 = (f32[256,1]{0,1:T(1,128)S(1)}, f32[256,1]{0,1:T(1,128)S(1)}, u32[]{:S(2)}, u32[]{:S(2)}) collective-permute-start(f32[256,1]{0,1:T(1,128)S(1)} %bitcast.109), channel_id=1, source_target_pairs={{0,1},{1,0},{2,3},{3,2},{4,5},{5,4},{6,7},{7,6},{8,9},{9,8},{10,11... | collective-permute-start | bytes 3080 | tf_op jit(solution)/shard_map/ppermute | solution.py:22
  123.3 43.8 %all-to-all-start.3 = ((bf16[8,32,2048]{2,1,0:T(8,128)(2,1)}), bf16[8,32,2048]{2,1,0:T(8,128)(2,1)S(1)}, u32[]{:S(2)}, u32[]{:S(2)}) async-start(bf16[8,32,2048]{2,1,0:T(8,128)(2,1)} %bitcast.94), calls=%async_computation.3 | async-start | bytes 2097152 | tf_op jit(solution)/shard_map/all_to_all | solution.py:18
  134.5 4.4 %collective-permute-start.7 = (f32[4,18,128]{2,1,0:T(8,128)S(1)}, f32[4,18,128]{2,1,0:T(8,128)S(1)}, u32[]{:S(2)}, u32[]{:S(2)}) collective-permute-start(f32[4,18,128]{2,1,0:T(8,128)S(1)} %get-tuple-element.14), channel_id=1, source_target_pairs={{24,0},{26,2},{28,4},{30,6},{0,8},{2,10},{4,12},{6,14},{8,16},{10,... | collective-permute-start | bytes 110600 | tf_op jit(solution)/shard_map/ppermute | solution.py:41
  135.7 5.7 %collective-permute-start.6 = (f32[4,18,128]{2,1,0:T(8,128)S(1)}, f32[4,18,128]{2,1,0:T(8,128)S(1)}, u32[]{:S(2)}, u32[]{:S(2)}) collective-permute-start(f32[4,18,128]{2,1,0:T(8,128)S(1)} %get-tuple-element.13), channel_id=1, source_target_pairs={{16,0},{18,2},{20,4},{22,6},{24,8},{26,10},{28,12},{30,14},{0,16},... | collective-permute-start | bytes 110600 | tf_op jit(solution)/shard_map/ppermute | solution.py:41
  138.5 4.1 %collective-permute-start.5 = (f32[4,18,128]{2,1,0:T(8,128)S(1)}, f32[4,18,128]{2,1,0:T(8,128)S(1)}, u32[]{:S(2)}, u32[]{:S(2)}) collective-permute-start(f32[4,18,128]{2,1,0:T(8,128)S(1)} %get-tuple-element.12), channel_id=1, source_target_pairs={{8,0},{10,2},{12,4},{14,6},{16,8},{18,10},{20,12},{22,14},{24,16},... | collective-permute-start | bytes 110600 | tf_op jit(solution)/shard_map/ppermute | solution.py:41
  142.6 4.2 %collective-permute-start.9 = (f32[4,18,128]{2,1,0:T(8,128)S(1)}, f32[4,18,128]{2,1,0:T(8,128)S(1)}, u32[]{:S(2)}, u32[]{:S(2)}) collective-permute-start(f32[4,18,128]{2,1,0:T(8,128)S(1)} %fusion.31), channel_id=1, source_target_pairs={{2,0},{4,2},{6,4},{0,6},{10,8},{12,10},{14,12},{8,14},{18,16},{20,... | collective-permute-start | bytes 110600 | tf_op jit(solution)/shard_map/ppermute | solution.py:46
  143.6 5.3 %collective-permute-start.10 = (f32[4,18,128]{2,1,0:T(8,128)S(1)}, f32[4,18,128]{2,1,0:T(8,128)S(1)}, u32[]{:S(2)}, u32[]{:S(2)}) collective-permute-start(f32[4,18,128]{2,1,0:T(8,128)S(1)} %fusion.31), channel_id=1, source_target_pairs={{6,0},{0,2},{2,4},{4,6},{14,8},{8,10},{10,12},{12,14},{22,16},{16,... | collective-permute-start | bytes 110600 | tf_op jit(solution)/shard_map/ppermute | solution.py:46
  144.7 5.6 %collective-permute-start.8 = (f32[4,18,128]{2,1,0:T(8,128)S(1)}, f32[4,18,128]{2,1,0:T(8,128)S(1)}, u32[]{:S(2)}, u32[]{:S(2)}) collective-permute-start(f32[4,18,128]{2,1,0:T(8,128)S(1)} %fusion.31), channel_id=1, source_target_pairs={{4,0},{6,2},{0,4},{2,6},{12,8},{14,10},{8,12},{10,14},{20,16},{22,... | collective-permute-start | bytes 110600 | tf_op jit(solution)/shard_map/ppermute | solution.py:46
  150.3 7.5 %collective-permute-start.12 = (f32[4,16,128]{2,1,0:T(8,128)S(1)}, f32[4,16,128]{2,1,0:T(8,128)S(1)}, u32[]{:S(2)}, u32[]{:S(2)}) collective-permute-start(f32[4,16,128]{2,1,0:T(8,128)S(1)} %slice.78), channel_id=1, source_target_pairs={{0,64},{32,96},{64,0},{96,32},{128,192},{160,224},{192,128},{224,1... | collective-permute-start | bytes 98312 | tf_op jit(solution)/shard_map/ppermute | solution.py:69
  153.3 5.8 %collective-permute-start.13 = (f32[4,16,128]{2,1,0:T(8,128)S(1)}, f32[4,16,128]{2,1,0:T(8,128)S(1)}, u32[]{:S(2)}, u32[]{:S(2)}) collective-permute-start(f32[4,16,128]{2,1,0:T(8,128)S(1)} %slice.78), channel_id=1, source_target_pairs={{0,96},{32,64},{64,32},{96,0},{128,224},{160,192},{192,160},{224,1... | collective-permute-start | bytes 98312 | tf_op jit(solution)/shard_map/ppermute | solution.py:69
  154.8 4.3 %collective-permute-start.11 = (f32[4,16,128]{2,1,0:T(8,128)S(1)}, f32[4,16,128]{2,1,0:T(8,128)S(1)}, u32[]{:S(2)}, u32[]{:S(2)}) collective-permute-start(f32[4,16,128]{2,1,0:T(8,128)S(1)} %slice.78), channel_id=1, source_target_pairs={{0,32},{32,0},{64,96},{96,64},{128,160},{160,128},{192,224},{224,1... | collective-permute-start | bytes 98312 | tf_op jit(solution)/shard_map/ppermute | solution.py:69
  159.1 7.9 %collective-permute-start.14 = (f32[4,16,128]{2,1,0:T(8,128)S(1)}, f32[4,16,128]{2,1,0:T(8,128)S(1)}, u32[]{:S(2)}, u32[]{:S(2)}) collective-permute-start(f32[4,16,128]{2,1,0:T(8,128)S(1)} %add_add_fusion.1.left_ref), channel_id=1, source_target_pairs={{0,128},{32,160},{64,192},{96,224},{128,0},{160,32},{192,64},{224,... | collective-permute-start | bytes 98312 | tf_op jit(solution)/shard_map/ppermute | solution.py:69
  167.0 6.6 %collective-permute-start.15 = (f32[4,16,128]{2,1,0:T(8,128)S(1)}, f32[4,16,128]{2,1,0:T(8,128)S(1)}, u32[]{:S(2)}, u32[]{:S(2)}) collective-permute-start(f32[4,16,128]{2,1,0:T(8,128)S(1)} %shard_map.94), channel_id=1, source_target_pairs={{8,0},{10,2},{12,4},{14,6},{16,8},{18,10},{20,12},{22,14},{24,16},... | collective-permute-start | bytes 98312 | tf_op jit(solution)/shard_map/ppermute | solution.py:41
  168.6 5.4 %collective-permute-start.16 = (f32[4,16,128]{2,1,0:T(8,128)S(1)}, f32[4,16,128]{2,1,0:T(8,128)S(1)}, u32[]{:S(2)}, u32[]{:S(2)}) collective-permute-start(f32[4,16,128]{2,1,0:T(8,128)S(1)} %shard_map.94), channel_id=1, source_target_pairs={{16,0},{18,2},{20,4},{22,6},{24,8},{26,10},{28,12},{30,14},{0,16},... | collective-permute-start | bytes 98312 | tf_op jit(solution)/shard_map/ppermute | solution.py:41
  169.3 4.7 %collective-permute-start.17 = (f32[4,16,128]{2,1,0:T(8,128)S(1)}, f32[4,16,128]{2,1,0:T(8,128)S(1)}, u32[]{:S(2)}, u32[]{:S(2)}) collective-permute-start(f32[4,16,128]{2,1,0:T(8,128)S(1)} %shard_map.94), channel_id=1, source_target_pairs={{24,0},{26,2},{28,4},{30,6},{0,8},{2,10},{4,12},{6,14},{8,16},{10,... | collective-permute-start | bytes 98312 | tf_op jit(solution)/shard_map/ppermute | solution.py:41
Sparse Core Ops, SparseCore 0:
  10.5 83.5 all-gather.1
